TPU v7x, 32 devices: a whole 2x2x4 slice. The times are simulated.
32 devices in a mesh: pipe: 4 (over x, core), ctx: 8 (over z, y).
Axes of the slice: x: 2, y: 2, z: 4, core: 2. Of those that a mesh axis runs over, the one named last changes fastest.
Arguments:
- queries: bfloat16 [2, 4, 1024, 2560], P(None, 'pipe', 'ctx'), may hold values from -80 to 80
- keys: bfloat16 [2, 4, 1024, 512], P(None, 'pipe', 'ctx'), may hold values from -25 to 25
- values: bfloat16 [2, 4, 1024, 512], P(None, 'pipe', 'ctx'), may hold values from -6 to 6
- grad_a: bfloat16 [4, 1024, 2560], P('pipe', 'ctx'), may hold values from -96 to 96
- grad_b: bfloat16 [4, 1024, 2560], P('pipe', 'ctx'), may hold values from -48 to 48
- imports: int32 [2, 4, 8, 8], P(None, 'pipe'), may hold values from 0 to 1, as said below
- block_ids: int32 [2, 4, 8], P(None, 'pipe'), may hold values from 0 to 7, each once within a row
Outputs:
- dq_a: bfloat16 [4, 1024, 2560], P('pipe', 'ctx')
- dq_b: bfloat16 [4, 1024, 2560], P('pipe', 'ctx')
- kv_grads: bfloat16 [2, 4, 1024, 1024], P(None, 'pipe', 'ctx')
Inputs may be any that keep to these rules, and one draw needn't show every extreme that they name: Every file block sees itself and imports at most 7 other blocks; in each micro-batch and section some block imports exactly 7.
All inputs are finite; a program needn't handle non-finite values.
Results may differ from a plain program's by a relative error of at most 0.015.
Values may be sent and summed in bfloat16 or wider, within the bound.
No kernel may reach another device: no remote copies, remote signals or barrier semaphores. Data moves between devices by JAX's collectives and lax.ppermute only.
A program may use at most 64 MiB of HBM per device.

v0:
```python
import math

import jax
import jax.numpy as jnp
from jax import lax
from jax.experimental import pallas as pl
from jax.experimental.pallas import tpu as pltpu
from jax.sharding import PartitionSpec as P

QUERY_HEADS = 20
KEY_VALUE_HEADS = 4
HEAD_DIMENSION = 128
FILE_BLOCK_SIZE = 128
MICRO_BATCHES = 2

GROUP = QUERY_HEADS // KEY_VALUE_HEADS
SIDES = 2
HALF_KV = KEY_VALUE_HEADS // SIDES
HALF_Q_WIDTH = HALF_KV * GROUP * HEAD_DIMENSION
HALF_KV_WIDTH = HALF_KV * HEAD_DIMENSION
STACK = GROUP * FILE_BLOCK_SIZE
negative_large = -1e30
SCALE = 1.0 / math.sqrt(HEAD_DIMENSION)
EXP2_SCALE = SCALE * math.log2(math.e)

NT = (((1,), (1,)), ((), ()))
NN = (((1,), (0,)), ((), ()))
TN = (((0,), (0,)), ((), ()))


def line_masks(lines):
    masks = []
    while lines > 1:
        masks.append(lines - 1)
        lines //= 2
    return masks


def line_offsets(lines):
    offsets = [0]
    for mask in line_masks(lines):
        offsets += [offset ^ mask for offset in offsets]
    return offsets


def fold_rows(tile, op):
    rows, columns = tile.shape
    return op(tile.reshape(rows // 8, 8, columns), axis=0)


def backward_kernel(lines, micro, with_arrived, kv_count, *refs):
    tiles = lines * SIDES
    refs = list(refs)
    imports_ref, ids_ref, q_ref, g_ref, received_ref = refs[:5]
    at = 5
    arrived_ref = None
    if with_arrived:
        arrived_ref = refs[at]
        at += 1
    kv_refs = refs[at : at + kv_count]
    at += kv_count
    dq_ref = refs[at]
    at += 1
    dkv_refs = refs[at : at + lines]
    at += lines
    packed, q_stack, g_stack, scores, dprobs, dkv_sum, listing = refs[at:]

    me = lax.axis_index("ctx")
    line, side = me // SIDES, lax.rem(me, SIDES)
    offsets = line_offsets(lines)
    lane = side * HALF_Q_WIDTH

    def tile_value(tile):
        if kv_count == tiles:
            return kv_refs[tile][...]
        return kv_refs[tile // SIDES][tile % SIDES]

    evens, chunks = [], []
    for block in range(SIDES):
        query_slot = line * SIDES + (side if block == 0 else 1 - side)
        query_id = ids_ref[micro, 0, query_slot]
        others = []
        total = jnp.int32(1)
        for tile in range(tiles):
            if tile == block:
                continue
            step, chain = tile // SIDES, tile % SIDES
            key_line = jnp.bitwise_xor(line, offsets[step])
            key_slot = key_line * SIDES + (side if chain == 0 else 1 - side)
            key_id = ids_ref[micro, 0, key_slot]
            live = imports_ref[micro, 0, query_id, key_id] > 0
            others.append((tile, live))
            total = total + jnp.where(live, 1, 0)
        even = lax.rem(total, 2) == 0
        evens.append(even)
        chunks.append((total + 1) // 2)
        listing[block, 0] = block
        listing[block, 1] = block
        packed[block, 0, :FILE_BLOCK_SIZE] = tile_value(block)
        packed[block, 0, FILE_BLOCK_SIZE:] = tile_value(block)
        place = jnp.where(even, 1, 2)
        for tile, live in others:

            def take(block=block, place=place, tile=tile):
                listing[block, place] = tile
                rows = pl.ds(
                    pl.multiple_of(lax.rem(place, 2) * FILE_BLOCK_SIZE, FILE_BLOCK_SIZE),
                    FILE_BLOCK_SIZE,
                )
                packed[block, place // 2, rows] = tile_value(tile)

            pl.when(live)(take)
            place = place + jnp.where(live, 1, 0)

    dkv_sum[...] = jnp.zeros_like(dkv_sum)

    triangle = lax.broadcasted_iota(jnp.int32, (FILE_BLOCK_SIZE, FILE_BLOCK_SIZE), 0) <= (
        lax.broadcasted_iota(jnp.int32, (FILE_BLOCK_SIZE, FILE_BLOCK_SIZE), 1)
    )
    allowed = jnp.concatenate([triangle] * GROUP, axis=1)
    head_columns = [
        slice(head * HEAD_DIMENSION, (head + 1) * HEAD_DIMENSION) for head in range(HALF_KV)
    ]
    value_columns = [
        slice(HALF_KV_WIDTH + head * HEAD_DIMENSION, HALF_KV_WIDTH + (head + 1) * HEAD_DIMENSION)
        for head in range(HALF_KV)
    ]

    for block in range(SIDES):
        for head in range(HALF_KV):
            for member in range(GROUP):
                rows = slice(member * FILE_BLOCK_SIZE, (member + 1) * FILE_BLOCK_SIZE)
                start = (head * GROUP + member) * HEAD_DIMENSION
                columns = slice(start, start + HEAD_DIMENSION)
                if block == 0:
                    wide = pl.ds(pl.multiple_of(lane + start, HEAD_DIMENSION), HEAD_DIMENSION)
                    q_stack[head, rows, :] = q_ref[micro, 0, :, wide]
                    upstream = g_ref[0, :, wide]
                else:
                    q_stack[head, rows, :] = received_ref[0, :, columns]
                    upstream = received_ref[1, :, columns]
                if with_arrived:
                    upstream = (
                        upstream.astype(jnp.float32)
                        + arrived_ref[block, :, columns].astype(jnp.float32)
                    ).astype(jnp.bfloat16)
                g_stack[head, rows, :] = upstream

        def products(chunk, head):
            score = lax.dot_general(
                packed[block, chunk, :, head_columns[head]],
                q_stack[head],
                NT,
                preferred_element_type=jnp.float32,
            )
            dprobs[head, chunk] = lax.dot_general(
                packed[block, chunk, :, value_columns[head]],
                g_stack[head],
                NT,
                preferred_element_type=jnp.float32,
            )
            return score

        def first(chunk, largest):
            found = []
            for head in range(HALF_KV):
                score = products(chunk, head)
                scores[head, chunk] = score
                found.append(jnp.maximum(largest[head], fold_rows(score, jnp.max)))
            return tuple(found)

        largest = []
        for head in range(HALF_KV):
            score = products(0, head)
            score = jnp.concatenate(
                [
                    jnp.where(allowed, score[:FILE_BLOCK_SIZE], negative_large),
                    score[FILE_BLOCK_SIZE:] + jnp.where(evens[block], 0.0, negative_large),
                ],
                axis=0,
            )
            scores[head, 0] = score
            largest.append(fold_rows(score, jnp.max))
        largest = lax.fori_loop(1, chunks[block], first, tuple(largest))
        row_max = [jnp.max(value, axis=0, keepdims=True) for value in largest]

        def second(chunk, sums):
            found = []
            for head in range(HALF_KV):
                weight = jnp.exp2((scores[head, chunk] - row_max[head]) * EXP2_SCALE)
                scores[head, chunk] = weight
                found.append(sums[2 * head] + fold_rows(weight, jnp.sum))
                found.append(sums[2 * head + 1] + fold_rows(weight * dprobs[head, chunk], jnp.sum))
            return tuple(found)

        nothing = jnp.zeros((8, STACK), jnp.float32)
        sums = lax.fori_loop(0, chunks[block], second, (nothing,) * (2 * HALF_KV))
        inverse = [1.0 / jnp.sum(sums[2 * h], axis=0, keepdims=True) for h in range(HALF_KV)]
        delta = [
            jnp.sum(sums[2 * h + 1], axis=0, keepdims=True) * inverse[h] for h in range(HALF_KV)
        ]

        def third(chunk, totals):
            found = []
            tile_pair = [listing[block, 2 * chunk], listing[block, 2 * chunk + 1]]
            for head in range(HALF_KV):
                prob = scores[head, chunk] * inverse[head]
                score_grad = (prob * (dprobs[head, chunk] - delta[head])).astype(jnp.bfloat16)
                key_part = lax.dot_general(
                    score_grad, q_stack[head], NN, preferred_element_type=jnp.float32
                )
                value_part = lax.dot_general(
                    prob.astype(jnp.bfloat16), g_stack[head], NN, preferred_element_type=jnp.float32
                )
                for place in range(2):
                    rows = slice(place * FILE_BLOCK_SIZE, (place + 1) * FILE_BLOCK_SIZE)
                    dkv_sum[tile_pair[place], :, head_columns[head]] += key_part[rows]
                    dkv_sum[tile_pair[place], :, value_columns[head]] += value_part[rows]
                found.append(
                    totals[head]
                    + lax.dot_general(
                        packed[block, chunk, :, head_columns[head]],
                        score_grad,
                        TN,
                        preferred_element_type=jnp.float32,
                    )
                )
            return tuple(found)

        empty = jnp.zeros((HEAD_DIMENSION, STACK), jnp.float32)
        dq_turned = lax.fori_loop(0, chunks[block], third, (empty,) * HALF_KV)
        for head in range(HALF_KV):
            for member in range(GROUP):
                start = (head * GROUP + member) * HEAD_DIMENSION
                part = dq_turned[head][:, member * FILE_BLOCK_SIZE : (member + 1) * FILE_BLOCK_SIZE]
                dq_ref[block, :, start : start + HEAD_DIMENSION] = (part.T * SCALE).astype(
                    jnp.bfloat16
                )

    for tile in range(tiles):
        out, chain = dkv_refs[tile // SIDES], tile % SIDES
        out[chain, :, :HALF_KV_WIDTH] = (dkv_sum[tile, :, :HALF_KV_WIDTH] * SCALE).astype(
            jnp.bfloat16
        )
        out[chain, :, HALF_KV_WIDTH:] = dkv_sum[tile, :, HALF_KV_WIDTH:].astype(jnp.bfloat16)


def backward(lines, micro, imports, block_ids, queries, gradient, received, arrived, kv_parts):
    tiles = lines * SIDES
    with_arrived = arrived is not None
    vmem = pl.BlockSpec(memory_space=pltpu.VMEM)
    smem = pl.BlockSpec(memory_space=pltpu.SMEM)
    operands = [imports, block_ids, queries, gradient, received]
    if with_arrived:
        operands.append(arrived)
    operands += kv_parts
    query_shape = (SIDES, FILE_BLOCK_SIZE, HALF_Q_WIDTH)
    key_shape = (SIDES, FILE_BLOCK_SIZE, 2 * HALF_KV_WIDTH)

    def body(*refs):
        backward_kernel(lines, micro, with_arrived, len(kv_parts), *refs)

    stacked = (HALF_KV, STACK, HEAD_DIMENSION)
    squares = (HALF_KV, tiles // 2, 2 * FILE_BLOCK_SIZE, STACK)
    scratch = [
        pltpu.VMEM((SIDES, tiles // 2, 2 * FILE_BLOCK_SIZE, 2 * HALF_KV_WIDTH), jnp.bfloat16),
        pltpu.VMEM(stacked, jnp.bfloat16),
        pltpu.VMEM(stacked, jnp.bfloat16),
        pltpu.VMEM(squares, jnp.float32),
        pltpu.VMEM(squares, jnp.float32),
        pltpu.VMEM((tiles, FILE_BLOCK_SIZE, 2 * HALF_KV_WIDTH), jnp.float32),
    ]
    needed = sum(math.prod(block.shape) * block.dtype.itemsize for block in scratch)
    needed += sum(math.prod(block.shape) * 2 for block in operands[2:])
    needed += math.prod(query_shape) * 2 + lines * math.prod(key_shape) * 2
    results = pl.pallas_call(
        body,
        out_shape=[jax.ShapeDtypeStruct(query_shape, jnp.bfloat16)]
        + [jax.ShapeDtypeStruct(key_shape, jnp.bfloat16)] * lines,
        in_specs=[smem, smem] + [vmem] * (len(operands) - 2),
        out_specs=[vmem] * (1 + lines),
        scratch_shapes=scratch + [pltpu.SMEM((SIDES, tiles), jnp.int32)],
        compiler_params=pltpu.CompilerParams(vmem_limit_bytes=needed + 6 * 1024 * 1024),
        cost_estimate=pl.CostEstimate(
            flops=10 * 10**9, bytes_accessed=4 * 10**6, transcendentals=0
        ),
    )(*operands)
    return results[0], results[1:]


def side_columns(of_side, width, start=0):
    return pl.ds(pl.multiple_of(start + of_side * width, HEAD_DIMENSION), width)


def my_side():
    return lax.rem(lax.axis_index("ctx"), SIDES)


def small_call(kernel, shapes, operands):
    vmem = pl.BlockSpec(memory_space=pltpu.VMEM)
    moved = sum(math.prod(block.shape) * 2 for block in operands)
    return pl.pallas_call(
        kernel,
        out_shape=[jax.ShapeDtypeStruct(shape, jnp.bfloat16) for shape in shapes],
        in_specs=[vmem] * len(operands),
        out_specs=[vmem] * len(shapes),
        compiler_params=pltpu.CompilerParams(vmem_limit_bytes=2 * moved + 4 * 1024 * 1024),
        cost_estimate=pl.CostEstimate(flops=0, bytes_accessed=2 * moved, transcendentals=0),
    )(*operands)


def split_keys_kernel(key_ref, value_ref, own_a_ref, own_b_ref, given_ref):
    side = my_side()
    own_refs = (own_a_ref, own_b_ref)
    for micro in range(MICRO_BATCHES):
        for place, ref in enumerate((key_ref, value_ref)):
            columns = slice(place * HALF_KV_WIDTH, (place + 1) * HALF_KV_WIDTH)
            own_refs[micro][:, columns] = ref[micro, 0, :, side_columns(side, HALF_KV_WIDTH)]
            given_ref[micro, :, columns] = ref[micro, 0, :, side_columns(1 - side, HALF_KV_WIDTH)]


def split_rows_kernel(micro, query_ref, gradient_ref, given_ref):
    columns = side_columns(1 - my_side(), HALF_Q_WIDTH)
    given_ref[0] = query_ref[micro, 0, :, columns]
    given_ref[1] = gradient_ref[0, :, columns]


def join_rows_kernel(own_ref, received_ref, out_ref):
    side = my_side()
    out_ref[0, :, side_columns(side, HALF_Q_WIDTH)] = own_ref[0]
    out_ref[0, :, side_columns(1 - side, HALF_Q_WIDTH)] = received_ref[...]


def assemble_kernel(sum_ref, crossed_ref, local_ref, *refs):
    *moved_refs, out_ref = refs
    half = len(moved_refs) // 2
    side = my_side()
    for micro in range(MICRO_BATCHES):
        if micro == 0:
            halves = (sum_ref[0], crossed_ref[...])
        else:
            halves = []
            for parts in (
                [local_ref[0]] + [ref[...] for ref in moved_refs[:half]],
                [ref[...] for ref in moved_refs[half:]],
            ):
                total = parts[0].astype(jnp.float32)
                for block in parts[1:]:
                    total = total + block.astype(jnp.float32)
                halves.append(total.astype(jnp.bfloat16))
        for total, of_side in zip(halves, (side, 1 - side)):
            for kind in range(2):
                start = kind * KEY_VALUE_HEADS * HEAD_DIMENSION
                out_ref[micro, 0, :, side_columns(of_side, HALF_KV_WIDTH, start)] = total[
                    :, kind * HALF_KV_WIDTH : (kind + 1) * HALF_KV_WIDTH
                ]


def on_device(queries, keys, values, grad_a, grad_b, imports, block_ids):
    devices = lax.axis_size("ctx")
    lines = devices // SIDES
    masks = line_masks(lines)
    offsets = line_offsets(lines)
    pipe = lax.axis_size("pipe")
    key_shape = (FILE_BLOCK_SIZE, 2 * HALF_KV_WIDTH)
    row_shape = (FILE_BLOCK_SIZE, HALF_Q_WIDTH)

    def moved(block, mask, crossing=0):
        route = [(i, i ^ (mask * SIDES + crossing)) for i in range(devices)]
        return lax.ppermute(block, "ctx", route)

    def swap(block):
        return moved(block, 0, 1)

    def down(block):
        return lax.ppermute(block, "pipe", [(i + 1, i) for i in range(pipe - 1)])

    def given_rows(micro, query_rows, gradient_rows):
        def kernel(*refs):
            split_rows_kernel(micro, *refs)

        return small_call(kernel, [(2,) + row_shape], [query_rows, gradient_rows])[0]

    def joined(own, received):
        shape = (1, FILE_BLOCK_SIZE, SIDES * HALF_Q_WIDTH)
        return small_call(join_rows_kernel, [shape], [own, received])[0]

    def together(*values):
        return list(lax.optimization_barrier(values))

    def add(*blocks):
        total = blocks[0].astype(jnp.float32)
        for block in blocks[1:]:
            total = total + block.astype(jnp.float32)
        return total.astype(jnp.bfloat16)

    def gathered(unit):
        units = [unit]
        for mask in masks:
            units += [moved(block, mask) for block in units]
        return units

    def nearer_sums(parts, last_waits=False):
        held = {offset: [part] for offset, part in zip(offsets, parts)}
        for level in range(len(masks) - 1, 0, -1):
            kept = offsets[: 1 << level]
            found = {}
            for offset in reversed(kept):
                near, far = add(*held[offset]), add(*held[offset ^ masks[level]])
                if offset == 0 and last_waits:
                    far = together(far, *found[masks[0]])[0]
                found[offset] = [near, moved(far, masks[level])]
            held = found
        return held

    own, own_b, given = small_call(
        split_keys_kernel, [key_shape, key_shape, (MICRO_BATCHES,) + key_shape], [keys, values]
    )
    others = swap(given)
    rows_a = swap(given_rows(0, queries, grad_a))
    tiles_a = []
    for pair in zip(gathered(own), gathered(others[0])):
        tiles_a += pair

    queries_b, gradient_b, _ = together(queries, grad_b, tiles_a[2])
    rows_b = swap(given_rows(1, queries_b, gradient_b))
    unit_b, rows_a, _ = together(jnp.stack([own_b, others[1]]), rows_a, tiles_a[3])
    early = [moved(unit_b, mask) for mask in masks]

    dq_a, dkv_a = backward(
        lines, 0, imports, block_ids, queries, grad_a, rows_a, None, tiles_a
    )
    dq_a, *rest = together(dq_a, *early, *dkv_a)
    early, dkv_a = rest[: len(masks)], rest[len(masks) :]
    arrived = down(dq_a)
    units_b = [unit_b]
    for mask, fresh in zip(masks, early):
        units_b += [fresh] + [moved(block, mask) for block in units_b[1:]]
    held_a = nearer_sums(dkv_a, True)
    far_a = add(*held_a[masks[0]])
    mirrored_a = moved(far_a, masks[0])
    near_a = held_a[0]
    back_a = swap(dq_a[1])
    dq_b, dkv_b = backward(
        lines, 1, imports, block_ids, queries, grad_b, rows_b, arrived, units_b
    )
    held_b = nearer_sums(dkv_b)
    near_b, back_a, mirrored_a, *near_a = together(
        held_b[masks[0]][-1], back_a, mirrored_a, *near_a
    )
    held_b[masks[0]][-1] = near_b
    far_b, local_b = add(*held_b[masks[0]]), add(*held_b[0])
    pieces_b = [
        local_b,
        moved(far_b[0], masks[0]),
        moved(far_b[1], masks[0], 1),
        swap(local_b[1]),
    ]
    sum_a = add(*near_a, mirrored_a)
    crossed_a = swap(sum_a[1])
    back_b = swap(dq_b[1])
    out_a = joined(dq_a, back_a)
    out_b = joined(dq_b, back_b)
    kv_shape = (MICRO_BATCHES, 1, FILE_BLOCK_SIZE, 2 * KEY_VALUE_HEADS * HEAD_DIMENSION)
    kv = small_call(assemble_kernel, [kv_shape], [sum_a, crossed_a, *pieces_b])[0]
    return out_a, out_b, kv


def solution(mesh):
    return jax.shard_map(
        on_device,
        mesh=mesh,
        in_specs=(
            P(None, "pipe", "ctx", None),
            P(None, "pipe", "ctx", None),
            P(None, "pipe", "ctx", None),
            P("pipe", "ctx", None),
            P("pipe", "ctx", None),
            P(None, "pipe", None, None),
            P(None, "pipe", None),
        ),
        out_specs=(P("pipe", "ctx", None), P("pipe", "ctx", None), P(None, "pipe", "ctx", None)),
        check_vma=False,
    )
```

profile of v0, /device:TPU:0, one launch (start us, length us, event | category | flops | bytes accessed | tf_op | source)
XLA Modules:
  0.0 90.8 jit_solution(9051243658043745853)
XLA Ops:
  0.6 0.9 %copy-done.5 = bf16[2,1,128,512]{3,2,1,0:T(8,128)(2,1)S(1)} copy-done((bf16[2,1,128,512]{3,2,1,0:T(8,128)(2,1)S(1)}, bf16[2,1,128,512]{3,2,1,0:T(8,128)(2,1)}, u32[]{:S(2)}) %copy-start.5) | copy-done | bytes 262168
  1.6 0.9 %copy-done.6 = bf16[2,1,128,512]{3,2,1,0:T(8,128)(2,1)S(1)} copy-done((bf16[2,1,128,512]{3,2,1,0:T(8,128)(2,1)S(1)}, bf16[2,1,128,512]{3,2,1,0:T(8,128)(2,1)}, u32[]{:S(2)}) %copy-start.6) | copy-done | bytes 262168
  2.6 3.0 %collective-permute-start = (bf16[2,128,512]{2,1,0:T(8,128)(2,1)S(1)}, bf16[2,128,512]{2,1,0:T(8,128)(2,1)S(1)}, u32[]{:S(2)}, u32[]{:S(2)}) collective-permute-start(bf16[2,128,512]{2,1,0:T(8,128)(2,1)S(1)} %get-tuple-element.34), channel_id=1, source_target_pairs={{0,1},{1,0},{2,3},{3,2},{4,5},{5,4},{6,7},{7,6},{8,9},{9,8},{10,11... | collective-permute-start | bytes 786440 | tf_op jit(solution)/shard_map/ppermute | solution.py:370
  5.6 1.3 %copy-done = bf16[2,1,128,2560]{3,2,1,0:T(8,128)(2,1)S(1)} copy-done((bf16[2,1,128,2560]{3,2,1,0:T(8,128)(2,1)S(1)}, bf16[2,1,128,2560]{3,2,1,0:T(8,128)(2,1)}, u32[]{:S(2)}) %copy-start) | copy-done | bytes 1310744
  6.9 1.1 %copy-done.2 = bf16[1,128,2560]{2,1,0:T(8,128)(2,1)S(1)} copy-done((bf16[1,128,2560]{2,1,0:T(8,128)(2,1)S(1)}, bf16[1,128,2560]{2,1,0:T(8,128)(2,1)}, u32[]{:S(2)}) %copy-start.2) | copy-done | bytes 655384
  8.1 0.1 collective-permute-start.1
  8.1 4.1 %collective-permute-start.3 = (bf16[128,512]{1,0:T(8,128)(2,1)S(1)}, bf16[128,512]{1,0:T(8,128)(2,1)S(1)}, u32[]{:S(2)}, u32[]{:S(2)}) collective-permute-start(bf16[128,512]{1,0:T(8,128)(2,1)S(1)} %get-tuple-element.36.refs_5_), channel_id=1, source_target_pairs={{0,6},{1,7},{2,4},{3,5},{4,2},{5,3},{6,0},{7,1},{8,14},{9,15},{10,... | collective-permute-start | bytes 393224 | tf_op jit(solution)/shard_map/ppermute | solution.py:370
  12.2 0.5 collective-permute-done
  12.8 0.0 copy-start.3
  12.8 0.0 copy-start.7
  12.8 0.0 copy-start.8
  12.8 4.2 %collective-permute-start.2 = (bf16[128,512]{1,0:T(8,128)(2,1)S(1)}, bf16[128,512]{1,0:T(8,128)(2,1)S(1)}, u32[]{:S(2)}, u32[]{:S(2)}) collective-permute-start(bf16[128,512]{1,0:T(8,128)(2,1)S(1)} %get-tuple-element.65.refs_6_), channel_id=1, source_target_pairs={{0,6},{1,7},{2,4},{3,5},{4,2},{5,3},{6,0},{7,1},{8,14},{9,15},{10,... | collective-permute-start | bytes 393224 | tf_op jit(solution)/shard_map/ppermute | solution.py:370
  17.0 0.0 collective-permute-start.4
  17.0 0.0 collective-permute-done.3.refs_7_
  17.0 4.0 %collective-permute-start.6 = (bf16[128,512]{1,0:T(8,128)(2,1)S(1)}, bf16[128,512]{1,0:T(8,128)(2,1)S(1)}, u32[]{:S(2)}, u32[]{:S(2)}) collective-permute-start(bf16[128,512]{1,0:T(8,128)(2,1)S(1)} %collective-permute-done.3.refs_7_), channel_id=1, source_target_pairs={{0,2},{1,3},{2,0},{3,1},{4,6},{5,7},{6,4},{7,5},{8,10},{9,11},{10,... | collective-permute-start | bytes 393224 | tf_op jit(solution)/shard_map/ppermute | solution.py:370
  21.0 0.0 collective-permute-start.5
  21.1 0.4 collective-permute-done.2.refs_8_
  21.4 1.9 %collective-permute-start.7 = (bf16[128,512]{1,0:T(8,128)(2,1)S(1)}, bf16[128,512]{1,0:T(8,128)(2,1)S(1)}, u32[]{:S(2)}, u32[]{:S(2)}) collective-permute-start(bf16[128,512]{1,0:T(8,128)(2,1)S(1)} %collective-permute-done.2.refs_8_), channel_id=1, source_target_pairs={{0,2},{1,3},{2,0},{3,1},{4,6},{5,7},{6,4},{7,5},{8,10},{9,11},{10,... | collective-permute-start | bytes 393224 | tf_op jit(solution)/shard_map/ppermute | solution.py:370
  23.4 2.6 %collective-permute-done.1.refs_4_ = bf16[2,128,1280]{2,1,0:T(8,128)(2,1)S(1)} collective-permute-done((bf16[2,128,1280]{2,1,0:T(8,128)(2,1)S(1)}, bf16[2,128,1280]{2,1,0:T(8,128)(2,1)S(1)}, u32[]{:S(2)}, u32[]{:S(2)}) %collective-permute-start.1) | collective-permute-done | bytes 655392 | tf_op jit(solution)/shard_map/ppermute | solution.py:370
  26.0 1.7 %collective-permute-start.10 = (bf16[2,128,1280]{2,1,0:T(8,128)(2,1)S(1)}, bf16[2,128,1280]{2,1,0:T(8,128)(2,1)S(1)}, u32[]{:S(2)}, u32[]{:S(2)}) collective-permute-start(bf16[2,128,1280]{2,1,0:T(8,128)(2,1)S(1)} %shard_map.97), channel_id=1, source_target_pairs={{0,1},{1,0},{2,3},{3,2},{4,5},{5,4},{6,7},{7,6},{8,9},{9,8},{10,11... | collective-permute-start | bytes 1966088 | tf_op jit(solution)/shard_map/ppermute | solution.py:370
  27.7 0.0 collective-permute-done.4.refs_9_
  27.7 3.6 %collective-permute-start.8 = (bf16[2,128,512]{2,1,0:T(8,128)(2,1)S(1)}, bf16[2,128,512]{2,1,0:T(8,128)(2,1)S(1)}, u32[]{:S(2)}, u32[]{:S(2)}) collective-permute-start(bf16[2,128,512]{2,1,0:T(8,128)(2,1)S(1)} %pad_maximum_fusion.refs_6_), channel_id=1, source_target_pairs={{0,6},{1,7},{2,4},{3,5},{4,2},{5,3},{6,0},{7,1},{8,14},{9,15},{10,... | collective-permute-start | bytes 786440 | tf_op jit(solution)/shard_map/ppermute | solution.py:370
  31.3 0.0 collective-permute-done.6.refs_11_
  31.3 0.0 collective-permute-start.9
  31.3 0.0 collective-permute-done.5.refs_10_
  31.3 0.0 collective-permute-done.7.refs_12_
  31.4 6.2 %shard_map.96 = (bf16[2,128,1280]{2,1,0:T(8,128)(2,1)S(1)}, bf16[2,128,512]{2,1,0:T(8,128)(2,1)S(1)}, bf16[2,128,512]{2,1,0:T(8,128)(2,1)S(1)}, bf16[2,128,512]{2,1,0:T(8,128)(2,1)S(1)}, bf16[2,128,512]{2,1,0:T(8,128)(2,1)S(1)}) custom-call(s32[2,1,8,8]{3,2,1,0:T(8,128)S(1)} %copy-done.7, s32[2,1,8]{2,1,0:T(1,128)S(1)} %copy-done.8, ...), custom_call_target="tpu_custom_call" | custom-call | flops 10000000000 | bytes 4000000 | tf_op jit(solution)/shard_map/pallas_call | solution.py:276
  37.5 1.2 %collective-permute-done.8.refs_7_ = bf16[2,128,512]{2,1,0:T(8,128)(2,1)S(1)} collective-permute-done((bf16[2,128,512]{2,1,0:T(8,128)(2,1)S(1)}, bf16[2,128,512]{2,1,0:T(8,128)(2,1)S(1)}, u32[]{:S(2)}, u32[]{:S(2)}) %collective-permute-start.8) | collective-permute-done | bytes 262176 | tf_op jit(solution)/shard_map/ppermute | solution.py:370
  38.7 3.4 %collective-permute-done.9.refs_8_ = bf16[2,128,512]{2,1,0:T(8,128)(2,1)S(1)} collective-permute-done((bf16[2,128,512]{2,1,0:T(8,128)(2,1)S(1)}, bf16[2,128,512]{2,1,0:T(8,128)(2,1)S(1)}, u32[]{:S(2)}, u32[]{:S(2)}) %collective-permute-start.9) | collective-permute-done | bytes 262176 | tf_op jit(solution)/shard_map/ppermute | solution.py:370
  42.2 3.5 %collective-permute-start.15 = (bf16[2,128,512]{2,1,0:T(8,128)(2,1)S(1)}, bf16[2,128,512]{2,1,0:T(8,128)(2,1)S(1)}, u32[]{:S(2)}, u32[]{:S(2)}) collective-permute-start(bf16[2,128,512]{2,1,0:T(8,128)(2,1)S(1)} %get-tuple-element.50), channel_id=1, source_target_pairs={{0,2},{1,3},{2,0},{3,1},{4,6},{5,7},{6,4},{7,5},{8,10},{9,11},{10,... | collective-permute-start | bytes 786440 | tf_op jit(solution)/shard_map/ppermute | solution.py:370
  45.7 1.3 %collective-permute-start.11 = (bf16[2,128,1280]{2,1,0:T(8,128)(2,1)S(1)}, bf16[2,128,1280]{2,1,0:T(8,128)(2,1)S(1)}, u32[]{:S(2)}, u32[]{:S(2)}) collective-permute-start(bf16[2,128,1280]{2,1,0:T(8,128)(2,1)S(1)} %get-tuple-element.43.own_ref), channel_id=1, source_target_pairs={{8,0},{16,8},{24,16},{9,1},{17,9},{25,17},{10,2},{18,10},{26,18},{... | collective-permute-start | bytes 1966088 | tf_op jit(solution)/shard_map/ppermute | solution.py:376
  47.0 0.1 collective-permute-start.12
  47.1 0.6 collective-permute-start.14
  47.6 2.9 %collective-permute-done.15 = bf16[2,128,512]{2,1,0:T(8,128)(2,1)S(1)} collective-permute-done((bf16[2,128,512]{2,1,0:T(8,128)(2,1)S(1)}, bf16[2,128,512]{2,1,0:T(8,128)(2,1)S(1)}, u32[]{:S(2)}, u32[]{:S(2)}) %collective-permute-start.15) | collective-permute-done | bytes 262176 | tf_op jit(solution)/shard_map/ppermute | solution.py:370
  50.5 2.5 %collective-permute-start.17 = (bf16[2,128,512]{2,1,0:T(8,128)(2,1)S(1)}, bf16[2,128,512]{2,1,0:T(8,128)(2,1)S(1)}, u32[]{:S(2)}, u32[]{:S(2)}) collective-permute-start(bf16[2,128,512]{2,1,0:T(8,128)(2,1)S(1)} %get-tuple-element.53), channel_id=1, source_target_pairs={{0,2},{1,3},{2,0},{3,1},{4,6},{5,7},{6,4},{7,5},{8,10},{9,11},{10,... | collective-permute-start | bytes 786440 | tf_op jit(solution)/shard_map/ppermute | solution.py:370
  53.0 0.1 add_convert_fusion.3
  53.1 0.0 collective-permute-done.10.refs_4_
  53.1 0.5 collective-permute-start.16
  53.6 2.6 %collective-permute-done.12.refs_9_ = bf16[2,128,512]{2,1,0:T(8,128)(2,1)S(1)} collective-permute-done((bf16[2,128,512]{2,1,0:T(8,128)(2,1)S(1)}, bf16[2,128,512]{2,1,0:T(8,128)(2,1)S(1)}, u32[]{:S(2)}, u32[]{:S(2)}) %collective-permute-start.12) | collective-permute-done | bytes 262176 | tf_op jit(solution)/shard_map/ppermute | solution.py:370
  56.1 0.0 collective-permute-done.11.refs_5_
  56.1 9.2 %shard_map.98 = (bf16[2,128,1280]{2,1,0:T(8,128)(2,1)S(1)}, bf16[2,128,512]{2,1,0:T(8,128)(2,1)S(1)}, bf16[2,128,512]{2,1,0:T(8,128)(2,1)S(1)}, bf16[2,128,512]{2,1,0:T(8,128)(2,1)S(1)}, bf16[2,128,512]{2,1,0:T(8,128)(2,1)S(1)}) custom-call(s32[2,1,8,8]{3,2,1,0:T(8,128)S(1)} %copy-done.7, s32[2,1,8]{2,1,0:T(1,128)S(1)} %copy-done.8, ...), custom_call_target="tpu_custom_call" | custom-call | flops 10000000000 | bytes 4000000 | tf_op jit(solution)/shard_map/pallas_call | solution.py:276
  65.3 4.1 %collective-permute-start.13 = (bf16[2,128,512]{2,1,0:T(8,128)(2,1)S(1)}, bf16[2,128,512]{2,1,0:T(8,128)(2,1)S(1)}, u32[]{:S(2)}, u32[]{:S(2)}) collective-permute-start(bf16[2,128,512]{2,1,0:T(8,128)(2,1)S(1)} %get-tuple-element.48), channel_id=1, source_target_pairs={{0,2},{1,3},{2,0},{3,1},{4,6},{5,7},{6,4},{7,5},{8,10},{9,11},{10,... | collective-permute-start | bytes 786440 | tf_op jit(solution)/shard_map/ppermute | solution.py:370
  69.4 0.1 collective-permute-start.20
  69.5 0.0 collective-permute-done.14.received_ref
  69.5 0.6 collective-permute-start.18
  70.1 0.0 collective-permute-done.17
  70.1 0.0 collective-permute-done.16
  70.1 6.5 %collective-permute-done.13 = bf16[2,128,512]{2,1,0:T(8,128)(2,1)S(1)} collective-permute-done((bf16[2,128,512]{2,1,0:T(8,128)(2,1)S(1)}, bf16[2,128,512]{2,1,0:T(8,128)(2,1)S(1)}, u32[]{:S(2)}, u32[]{:S(2)}) %collective-permute-start.13) | collective-permute-done | bytes 262176 | tf_op jit(solution)/shard_map/ppermute | solution.py:370
  76.6 0.1 add_convert_fusion
  76.7 0.9 collective-permute-start.21
  77.6 3.0 %collective-permute-start.22 = (bf16[128,512]{1,0:T(8,128)(2,1)S(1)}, bf16[128,512]{1,0:T(8,128)(2,1)S(1)}, u32[]{:S(2)}, u32[]{:S(2)}) collective-permute-start(bf16[128,512]{1,0:T(8,128)(2,1)S(1)} %get-tuple-element.63), channel_id=1, source_target_pairs={{0,7},{1,6},{2,5},{3,4},{4,3},{5,2},{6,1},{7,0},{8,15},{9,14},{10,... | collective-permute-start | bytes 393224 | tf_op jit(solution)/shard_map/ppermute | solution.py:370
  80.6 0.0 collective-permute-done.20
  80.6 0.1 add_convert_fusion.1.local_ref
  80.7 1.6 %collective-permute-start.23 = (bf16[128,512]{1,0:T(8,128)(2,1)S(1)}, bf16[128,512]{1,0:T(8,128)(2,1)S(1)}, u32[]{:S(2)}, u32[]{:S(2)}) collective-permute-start(bf16[128,512]{1,0:T(8,128)(2,1)S(1)} %slice_bitcast_fusion.2), channel_id=1, source_target_pairs={{0,1},{1,0},{2,3},{3,2},{4,5},{5,4},{6,7},{7,6},{8,9},{9,8},{10,11... | collective-permute-start | bytes 393224 | tf_op jit(solution)/shard_map/ppermute | solution.py:370
  82.3 0.1 add_convert_fusion.2.sum_ref
  82.4 0.6 collective-permute-start.19
  82.9 0.9 shard_map.99
  83.8 0.0 collective-permute-done.18.received_ref
  83.9 0.9 shard_map.100
  84.8 0.3 collective-permute-done.21.refs_0_
  85.1 2.8 %collective-permute-done.22.refs_1_ = bf16[128,512]{1,0:T(8,128)(2,1)S(1)} collective-permute-done((bf16[128,512]{1,0:T(8,128)(2,1)S(1)}, bf16[128,512]{1,0:T(8,128)(2,1)S(1)}, u32[]{:S(2)}, u32[]{:S(2)}) %collective-permute-start.22) | collective-permute-done | bytes 131104 | tf_op jit(solution)/shard_map/ppermute | solution.py:370
  87.9 0.6 collective-permute-done.23.refs_2_
  88.5 1.4 %collective-permute-done.19.crossed_ref = bf16[128,512]{1,0:T(8,128)(2,1)S(1)} collective-permute-done((bf16[128,512]{1,0:T(8,128)(2,1)S(1)}, bf16[128,512]{1,0:T(8,128)(2,1)S(1)}, u32[]{:S(2)}, u32[]{:S(2)}) %collective-permute-start.19) | collective-permute-done | bytes 131104 | tf_op jit(solution)/shard_map/ppermute | solution.py:370
  89.9 0.9 shard_map.101
  (21 shorter events, 0.3 us)
Async XLA Ops:
  0.6 1.0 %copy-start.5 = (bf16[2,1,128,512]{3,2,1,0:T(8,128)(2,1)S(1)}, bf16[2,1,128,512]{3,2,1,0:T(8,128)(2,1)}, u32[]{:S(2)}) copy-start(bf16[2,1,128,512]{3,2,1,0:T(8,128)(2,1)} %key_ref.1) | copy-start | bytes 786436
  1.6 0.9 %copy-start.6 = (bf16[2,1,128,512]{3,2,1,0:T(8,128)(2,1)S(1)}, bf16[2,1,128,512]{3,2,1,0:T(8,128)(2,1)}, u32[]{:S(2)}) copy-start(bf16[2,1,128,512]{3,2,1,0:T(8,128)(2,1)} %value_ref.1) | copy-start | bytes 786436
  2.6 10.2 %collective-permute-start = (bf16[2,128,512]{2,1,0:T(8,128)(2,1)S(1)}, bf16[2,128,512]{2,1,0:T(8,128)(2,1)S(1)}, u32[]{:S(2)}, u32[]{:S(2)}) collective-permute-start(bf16[2,128,512]{2,1,0:T(8,128)(2,1)S(1)} %get-tuple-element.34), channel_id=1, source_target_pairs={{0,1},{1,0},{2,3},{3,2},{4,5},{5,4},{6,7},{7,6},{8,9},{9,8},{10,11... | collective-permute-start | bytes 786440 | tf_op jit(solution)/shard_map/ppermute | solution.py:370
  5.6 1.3 %copy-start = (bf16[2,1,128,2560]{3,2,1,0:T(8,128)(2,1)S(1)}, bf16[2,1,128,2560]{3,2,1,0:T(8,128)(2,1)}, u32[]{:S(2)}) copy-start(bf16[2,1,128,2560]{3,2,1,0:T(8,128)(2,1)} %refs_2_.3) | copy-start | bytes 3932164
  6.9 1.1 %copy-start.2 = (bf16[1,128,2560]{2,1,0:T(8,128)(2,1)S(1)}, bf16[1,128,2560]{2,1,0:T(8,128)(2,1)}, u32[]{:S(2)}) copy-start(bf16[1,128,2560]{2,1,0:T(8,128)(2,1)} %refs_3_.2) | copy-start | bytes 1966084
  8.0 15.3 %copy-start.1 = (bf16[2,1,128,2560]{3,2,1,0:T(8,128)(2,1)S(1)}, bf16[2,1,128,2560]{3,2,1,0:T(8,128)(2,1)}, u32[]{:S(2)}) copy-start(bf16[2,1,128,2560]{3,2,1,0:T(8,128)(2,1)} %refs_2_.3) | copy-start | bytes 3932164
  8.0 15.3 %copy-start.4 = (bf16[1,128,2560]{2,1,0:T(8,128)(2,1)S(1)}, bf16[1,128,2560]{2,1,0:T(8,128)(2,1)}, u32[]{:S(2)}) copy-start(bf16[1,128,2560]{2,1,0:T(8,128)(2,1)} %refs_3_.3) | copy-start | bytes 1966084
  8.1 17.9 %collective-permute-start.1 = (bf16[2,128,1280]{2,1,0:T(8,128)(2,1)S(1)}, bf16[2,128,1280]{2,1,0:T(8,128)(2,1)S(1)}, u32[]{:S(2)}, u32[]{:S(2)}) collective-permute-start(bf16[2,128,1280]{2,1,0:T(8,128)(2,1)S(1)} %shard_map.95), channel_id=1, source_target_pairs={{0,1},{1,0},{2,3},{3,2},{4,5},{5,4},{6,7},{7,6},{8,9},{9,8},{10,11... | collective-permute-start | bytes 1966088 | tf_op jit(solution)/shard_map/ppermute | solution.py:370
  8.1 8.9 %collective-permute-start.3 = (bf16[128,512]{1,0:T(8,128)(2,1)S(1)}, bf16[128,512]{1,0:T(8,128)(2,1)S(1)}, u32[]{:S(2)}, u32[]{:S(2)}) collective-permute-start(bf16[128,512]{1,0:T(8,128)(2,1)S(1)} %get-tuple-element.36.refs_5_), channel_id=1, source_target_pairs={{0,6},{1,7},{2,4},{3,5},{4,2},{5,3},{6,0},{7,1},{8,14},{9,15},{10,... | collective-permute-start | bytes 393224 | tf_op jit(solution)/shard_map/ppermute | solution.py:370
  12.8 18.6 %copy-start.3 = (bf16[1,128,2560]{2,1,0:T(8,128)(2,1)S(1)}, bf16[1,128,2560]{2,1,0:T(8,128)(2,1)}, u32[]{:S(2)}) copy-start(bf16[1,128,2560]{2,1,0:T(8,128)(2,1)} %refs_3_.2) | copy-start | bytes 1966084
  12.8 18.6 %copy-start.7 = (s32[2,1,8,8]{3,2,1,0:T(8,128)S(1)}, s32[2,1,8,8]{3,2,1,0:T(8,128)}, u32[]{:S(2)}) copy-start(s32[2,1,8,8]{3,2,1,0:T(8,128)} %refs_0_.6) | copy-start | bytes 1540
  12.8 18.6 %copy-start.8 = (s32[2,1,8]{2,1,0:T(1,128)S(1)}, s32[2,1,8]{2,1,0:T(1,128)}, u32[]{:S(2)}) copy-start(s32[2,1,8]{2,1,0:T(1,128)} %refs_1_.6) | copy-start | bytes 196
  12.8 8.6 %collective-permute-start.2 = (bf16[128,512]{1,0:T(8,128)(2,1)S(1)}, bf16[128,512]{1,0:T(8,128)(2,1)S(1)}, u32[]{:S(2)}, u32[]{:S(2)}) collective-permute-start(bf16[128,512]{1,0:T(8,128)(2,1)S(1)} %get-tuple-element.65.refs_6_), channel_id=1, source_target_pairs={{0,6},{1,7},{2,4},{3,5},{4,2},{5,3},{6,0},{7,1},{8,14},{9,15},{10,... | collective-permute-start | bytes 393224 | tf_op jit(solution)/shard_map/ppermute | solution.py:370
  17.0 10.7 %collective-permute-start.4 = (bf16[128,512]{1,0:T(8,128)(2,1)S(1)}, bf16[128,512]{1,0:T(8,128)(2,1)S(1)}, u32[]{:S(2)}, u32[]{:S(2)}) collective-permute-start(bf16[128,512]{1,0:T(8,128)(2,1)S(1)} %get-tuple-element.36.refs_5_), channel_id=1, source_target_pairs={{0,2},{1,3},{2,0},{3,1},{4,6},{5,7},{6,4},{7,5},{8,10},{9,11},{10,... | collective-permute-start | bytes 393224 | tf_op jit(solution)/shard_map/ppermute | solution.py:370
  17.0 14.3 %collective-permute-start.6 = (bf16[128,512]{1,0:T(8,128)(2,1)S(1)}, bf16[128,512]{1,0:T(8,128)(2,1)S(1)}, u32[]{:S(2)}, u32[]{:S(2)}) collective-permute-start(bf16[128,512]{1,0:T(8,128)(2,1)S(1)} %collective-permute-done.3.refs_7_), channel_id=1, source_target_pairs={{0,2},{1,3},{2,0},{3,1},{4,6},{5,7},{6,4},{7,5},{8,10},{9,11},{10,... | collective-permute-start | bytes 393224 | tf_op jit(solution)/shard_map/ppermute | solution.py:370
  21.0 10.3 %collective-permute-start.5 = (bf16[128,512]{1,0:T(8,128)(2,1)S(1)}, bf16[128,512]{1,0:T(8,128)(2,1)S(1)}, u32[]{:S(2)}, u32[]{:S(2)}) collective-permute-start(bf16[128,512]{1,0:T(8,128)(2,1)S(1)} %get-tuple-element.65.refs_6_), channel_id=1, source_target_pairs={{0,2},{1,3},{2,0},{3,1},{4,6},{5,7},{6,4},{7,5},{8,10},{9,11},{10,... | collective-permute-start | bytes 393224 | tf_op jit(solution)/shard_map/ppermute | solution.py:370
  21.4 9.9 %collective-permute-start.7 = (bf16[128,512]{1,0:T(8,128)(2,1)S(1)}, bf16[128,512]{1,0:T(8,128)(2,1)S(1)}, u32[]{:S(2)}, u32[]{:S(2)}) collective-permute-start(bf16[128,512]{1,0:T(8,128)(2,1)S(1)} %collective-permute-done.2.refs_8_), channel_id=1, source_target_pairs={{0,2},{1,3},{2,0},{3,1},{4,6},{5,7},{6,4},{7,5},{8,10},{9,11},{10,... | collective-permute-start | bytes 393224 | tf_op jit(solution)/shard_map/ppermute | solution.py:370
  26.0 27.1 %collective-permute-start.10 = (bf16[2,128,1280]{2,1,0:T(8,128)(2,1)S(1)}, bf16[2,128,1280]{2,1,0:T(8,128)(2,1)S(1)}, u32[]{:S(2)}, u32[]{:S(2)}) collective-permute-start(bf16[2,128,1280]{2,1,0:T(8,128)(2,1)S(1)} %shard_map.97), channel_id=1, source_target_pairs={{0,1},{1,0},{2,3},{3,2},{4,5},{5,4},{6,7},{7,6},{8,9},{9,8},{10,11... | collective-permute-start | bytes 1966088 | tf_op jit(solution)/shard_map/ppermute | solution.py:370
  27.7 11.0 %collective-permute-start.8 = (bf16[2,128,512]{2,1,0:T(8,128)(2,1)S(1)}, bf16[2,128,512]{2,1,0:T(8,128)(2,1)S(1)}, u32[]{:S(2)}, u32[]{:S(2)}) collective-permute-start(bf16[2,128,512]{2,1,0:T(8,128)(2,1)S(1)} %pad_maximum_fusion.refs_6_), channel_id=1, source_target_pairs={{0,6},{1,7},{2,4},{3,5},{4,2},{5,3},{6,0},{7,1},{8,14},{9,15},{10,... | collective-permute-start | bytes 786440 | tf_op jit(solution)/shard_map/ppermute | solution.py:370
  31.3 10.9 %collective-permute-start.9 = (bf16[2,128,512]{2,1,0:T(8,128)(2,1)S(1)}, bf16[2,128,512]{2,1,0:T(8,128)(2,1)S(1)}, u32[]{:S(2)}, u32[]{:S(2)}) collective-permute-start(bf16[2,128,512]{2,1,0:T(8,128)(2,1)S(1)} %pad_maximum_fusion.refs_6_), channel_id=1, source_target_pairs={{0,2},{1,3},{2,0},{3,1},{4,6},{5,7},{6,4},{7,5},{8,10},{9,11},{10,... | collective-permute-start | bytes 786440 | tf_op jit(solution)/shard_map/ppermute | solution.py:370
  42.2 8.3 %collective-permute-start.15 = (bf16[2,128,512]{2,1,0:T(8,128)(2,1)S(1)}, bf16[2,128,512]{2,1,0:T(8,128)(2,1)S(1)}, u32[]{:S(2)}, u32[]{:S(2)}) collective-permute-start(bf16[2,128,512]{2,1,0:T(8,128)(2,1)S(1)} %get-tuple-element.50), channel_id=1, source_target_pairs={{0,2},{1,3},{2,0},{3,1},{4,6},{5,7},{6,4},{7,5},{8,10},{9,11},{10,... | collective-permute-start | bytes 786440 | tf_op jit(solution)/shard_map/ppermute | solution.py:370
  45.7 10.5 %collective-permute-start.11 = (bf16[2,128,1280]{2,1,0:T(8,128)(2,1)S(1)}, bf16[2,128,1280]{2,1,0:T(8,128)(2,1)S(1)}, u32[]{:S(2)}, u32[]{:S(2)}) collective-permute-start(bf16[2,128,1280]{2,1,0:T(8,128)(2,1)S(1)} %get-tuple-element.43.own_ref), channel_id=1, source_target_pairs={{8,0},{16,8},{24,16},{9,1},{17,9},{25,17},{10,2},{18,10},{26,18},{... | collective-permute-start | bytes 1966088 | tf_op jit(solution)/shard_map/ppermute | solution.py:376
  47.0 9.2 %collective-permute-start.12 = (bf16[2,128,512]{2,1,0:T(8,128)(2,1)S(1)}, bf16[2,128,512]{2,1,0:T(8,128)(2,1)S(1)}, u32[]{:S(2)}, u32[]{:S(2)}) collective-permute-start(bf16[2,128,512]{2,1,0:T(8,128)(2,1)S(1)} %collective-permute-done.8.refs_7_), channel_id=1, source_target_pairs={{0,2},{1,3},{2,0},{3,1},{4,6},{5,7},{6,4},{7,5},{8,10},{9,11},{10,... | collective-permute-start | bytes 786440 | tf_op jit(solution)/shard_map/ppermute | solution.py:370
  47.1 22.4 %collective-permute-start.14 = (bf16[128,1280]{1,0:T(8,128)(2,1)S(1)}, bf16[128,1280]{1,0:T(8,128)(2,1)S(1)}, u32[]{:S(2)}, u32[]{:S(2)}) collective-permute-start(bf16[128,1280]{1,0:T(8,128)(2,1)S(1)} %slice_bitcast_fusion.1), channel_id=1, source_target_pairs={{0,1},{1,0},{2,3},{3,2},{4,5},{5,4},{6,7},{7,6},{8,9},{9,8},{10,11... | collective-permute-start | bytes 983048 | tf_op jit(solution)/shard_map/ppermute | solution.py:370
  50.5 19.6 %collective-permute-start.17 = (bf16[2,128,512]{2,1,0:T(8,128)(2,1)S(1)}, bf16[2,128,512]{2,1,0:T(8,128)(2,1)S(1)}, u32[]{:S(2)}, u32[]{:S(2)}) collective-permute-start(bf16[2,128,512]{2,1,0:T(8,128)(2,1)S(1)} %get-tuple-element.53), channel_id=1, source_target_pairs={{0,2},{1,3},{2,0},{3,1},{4,6},{5,7},{6,4},{7,5},{8,10},{9,11},{10,... | collective-permute-start | bytes 786440 | tf_op jit(solution)/shard_map/ppermute | solution.py:370
  53.1 17.0 %collective-permute-start.16 = (bf16[2,128,512]{2,1,0:T(8,128)(2,1)S(1)}, bf16[2,128,512]{2,1,0:T(8,128)(2,1)S(1)}, u32[]{:S(2)}, u32[]{:S(2)}) collective-permute-start(bf16[2,128,512]{2,1,0:T(8,128)(2,1)S(1)} %add_convert_fusion.3), channel_id=1, source_target_pairs={{0,6},{1,7},{2,4},{3,5},{4,2},{5,3},{6,0},{7,1},{8,14},{9,15},{10,... | collective-permute-start | bytes 786440 | tf_op jit(solution)/shard_map/ppermute | solution.py:370
  65.3 11.3 %collective-permute-start.13 = (bf16[2,128,512]{2,1,0:T(8,128)(2,1)S(1)}, bf16[2,128,512]{2,1,0:T(8,128)(2,1)S(1)}, u32[]{:S(2)}, u32[]{:S(2)}) collective-permute-start(bf16[2,128,512]{2,1,0:T(8,128)(2,1)S(1)} %get-tuple-element.48), channel_id=1, source_target_pairs={{0,2},{1,3},{2,0},{3,1},{4,6},{5,7},{6,4},{7,5},{8,10},{9,11},{10,... | collective-permute-start | bytes 786440 | tf_op jit(solution)/shard_map/ppermute | solution.py:370
  69.4 11.2 %collective-permute-start.20 = (bf16[2,128,512]{2,1,0:T(8,128)(2,1)S(1)}, bf16[2,128,512]{2,1,0:T(8,128)(2,1)S(1)}, u32[]{:S(2)}, u32[]{:S(2)}) collective-permute-start(bf16[2,128,512]{2,1,0:T(8,128)(2,1)S(1)} %get-tuple-element.60), channel_id=1, source_target_pairs={{0,2},{1,3},{2,0},{3,1},{4,6},{5,7},{6,4},{7,5},{8,10},{9,11},{10,... | collective-permute-start | bytes 786440 | tf_op jit(solution)/shard_map/ppermute | solution.py:370
  69.5 14.3 %collective-permute-start.18 = (bf16[128,1280]{1,0:T(8,128)(2,1)S(1)}, bf16[128,1280]{1,0:T(8,128)(2,1)S(1)}, u32[]{:S(2)}, u32[]{:S(2)}) collective-permute-start(bf16[128,1280]{1,0:T(8,128)(2,1)S(1)} %slice_bitcast_fusion), channel_id=1, source_target_pairs={{0,1},{1,0},{2,3},{3,2},{4,5},{5,4},{6,7},{7,6},{8,9},{9,8},{10,11... | collective-permute-start | bytes 983048 | tf_op jit(solution)/shard_map/ppermute | solution.py:370
  76.7 8.4 %collective-permute-start.21 = (bf16[128,512]{1,0:T(8,128)(2,1)S(1)}, bf16[128,512]{1,0:T(8,128)(2,1)S(1)}, u32[]{:S(2)}, u32[]{:S(2)}) collective-permute-start(bf16[128,512]{1,0:T(8,128)(2,1)S(1)} %get-tuple-element.64), channel_id=1, source_target_pairs={{0,6},{1,7},{2,4},{3,5},{4,2},{5,3},{6,0},{7,1},{8,14},{9,15},{10,... | collective-permute-start | bytes 393224 | tf_op jit(solution)/shard_map/ppermute | solution.py:370
  77.6 10.3 %collective-permute-start.22 = (bf16[128,512]{1,0:T(8,128)(2,1)S(1)}, bf16[128,512]{1,0:T(8,128)(2,1)S(1)}, u32[]{:S(2)}, u32[]{:S(2)}) collective-permute-start(bf16[128,512]{1,0:T(8,128)(2,1)S(1)} %get-tuple-element.63), channel_id=1, source_target_pairs={{0,7},{1,6},{2,5},{3,4},{4,3},{5,2},{6,1},{7,0},{8,15},{9,14},{10,... | collective-permute-start | bytes 393224 | tf_op jit(solution)/shard_map/ppermute | solution.py:370
  80.7 7.8 %collective-permute-start.23 = (bf16[128,512]{1,0:T(8,128)(2,1)S(1)}, bf16[128,512]{1,0:T(8,128)(2,1)S(1)}, u32[]{:S(2)}, u32[]{:S(2)}) collective-permute-start(bf16[128,512]{1,0:T(8,128)(2,1)S(1)} %slice_bitcast_fusion.2), channel_id=1, source_target_pairs={{0,1},{1,0},{2,3},{3,2},{4,5},{5,4},{6,7},{7,6},{8,9},{9,8},{10,11... | collective-permute-start | bytes 393224 | tf_op jit(solution)/shard_map/ppermute | solution.py:370
  82.4 7.5 %collective-permute-start.19 = (bf16[128,512]{1,0:T(8,128)(2,1)S(1)}, bf16[128,512]{1,0:T(8,128)(2,1)S(1)}, u32[]{:S(2)}, u32[]{:S(2)}) collective-permute-start(bf16[128,512]{1,0:T(8,128)(2,1)S(1)} %slice_bitcast_fusion.5), channel_id=1, source_target_pairs={{0,1},{1,0},{2,3},{3,2},{4,5},{5,4},{6,7},{7,6},{8,9},{9,8},{10,11... | collective-permute-start | bytes 393224 | tf_op jit(solution)/shard_map/ppermute | solution.py:370
where the time goes:
time: 92.3 us; the launch traced here: 90.8 us
  starting transfers between devices  41.8 us (45%)
  waiting for transfers between devices  25.2 us (27%)
  Pallas kernels  18.2 us (20%)
  local copies, waits for them, and re-layouts  4.42 us (5%)
    ppermute x23, starting transfers between devices, moved(): return lax.ppermute(block, 'ctx', route)  40.5 us
    ppermute x23, waiting for transfers between devices, moved(): return lax.ppermute(block, 'ctx', route)  25.2 us
    pallas_call x2, Pallas kernels, backward(): pl.pallas_call(body, out_shape=[jax.ShapeDtypeStruct(query_shape, jnp.bfl...  15.4 us
    unnamed x18, local copies, waits for them, and re-layouts  4.32 us
    pallas_call x6, Pallas kernels, small_call(): pl.pallas_call(kernel, out_shape=[jax.ShapeDtypeStruct(shape, jnp.bfloat1...  2.8 us
  transfers between devices with their start and end apart: 24, of which 12 were waited for; matrix products, arithmetic and copies ran while one was open for 0% of the time, Pallas kernels for 19%

commit v1 on v0

--- a/solution.py
+++ b/solution.py
@@ -63,7 +63,7 @@
     at += 1
     dkv_refs = refs[at : at + lines]
     at += lines
-    packed, q_stack, g_stack, scores, dprobs, dkv_sum, listing = refs[at:]
+    packed, q_stack, g_stack, scores, dprobs, dkv_sum, dq_sum, listing = refs[at:]
 
     me = lax.axis_index("ctx")
     line, side = me // SIDES, lax.rem(me, SIDES)
@@ -200,8 +200,7 @@
             jnp.sum(sums[2 * h + 1], axis=0, keepdims=True) * inverse[h] for h in range(HALF_KV)
         ]
 
-        def third(chunk, totals):
-            found = []
+        def third(chunk, carried):
             tile_pair = [listing[block, 2 * chunk], listing[block, 2 * chunk + 1]]
             for head in range(HALF_KV):
                 prob = scores[head, chunk] * inverse[head]
@@ -216,19 +215,17 @@
                     rows = slice(place * FILE_BLOCK_SIZE, (place + 1) * FILE_BLOCK_SIZE)
                     dkv_sum[tile_pair[place], :, head_columns[head]] += key_part[rows]
                     dkv_sum[tile_pair[place], :, value_columns[head]] += value_part[rows]
-                found.append(
-                    totals[head]
-                    + lax.dot_general(
-                        packed[block, chunk, :, head_columns[head]],
-                        score_grad,
-                        TN,
-                        preferred_element_type=jnp.float32,
-                    )
+                dq_sum[head] += lax.dot_general(
+                    packed[block, chunk, :, head_columns[head]],
+                    score_grad,
+                    TN,
+                    preferred_element_type=jnp.float32,
                 )
-            return tuple(found)
-
-        empty = jnp.zeros((HEAD_DIMENSION, STACK), jnp.float32)
-        dq_turned = lax.fori_loop(0, chunks[block], third, (empty,) * HALF_KV)
+            return carried
+
+        dq_sum[...] = jnp.zeros_like(dq_sum)
+        lax.fori_loop(0, chunks[block], third, 0)
+        dq_turned = [dq_sum[head] for head in range(HALF_KV)]
         for head in range(HALF_KV):
             for member in range(GROUP):
                 start = (head * GROUP + member) * HEAD_DIMENSION
@@ -269,6 +266,7 @@
         pltpu.VMEM(squares, jnp.float32),
         pltpu.VMEM(squares, jnp.float32),
         pltpu.VMEM((tiles, FILE_BLOCK_SIZE, 2 * HALF_KV_WIDTH), jnp.float32),
+        pltpu.VMEM((HALF_KV, HEAD_DIMENSION, STACK), jnp.float32),
     ]
     needed = sum(math.prod(block.shape) * block.dtype.itemsize for block in scratch)
     needed += sum(math.prod(block.shape) * 2 for block in operands[2:])
@@ -422,9 +420,9 @@
     for pair in zip(gathered(own), gathered(others[0])):
         tiles_a += pair
 
-    queries_b, gradient_b, _ = together(queries, grad_b, tiles_a[2])
+    queries_b, gradient_b, _ = together(queries, grad_b, tiles_a[3])
     rows_b = swap(given_rows(1, queries_b, gradient_b))
-    unit_b, rows_a, _ = together(jnp.stack([own_b, others[1]]), rows_a, tiles_a[3])
+    unit_b, rows_a, _ = together(jnp.stack([own_b, others[1]]), rows_a, tiles_a[4])
     early = [moved(unit_b, mask) for mask in masks]
 
     dq_a, dkv_a = backward(
@@ -436,7 +434,7 @@
     units_b = [unit_b]
     for mask, fresh in zip(masks, early):
         units_b += [fresh] + [moved(block, mask) for block in units_b[1:]]
-    held_a = nearer_sums(dkv_a, True)
+    held_a = nearer_sums(dkv_a)
     far_a = add(*held_a[masks[0]])
     mirrored_a = moved(far_a, masks[0])
     near_a = held_a[0]

time: 92.3 us -> 90 us (0.975); the launches traced: 90.8 us -> 90.1 us
  Pallas kernels: 18.2 us -> 15.7 us
  waiting for transfers between devices: 25.2 us -> 26.9 us
    pallas_call x2, Pallas kernels: 15.4 us -> 12.9 us  [backward(): pl.pallas_call(body, out_shape=[jax.ShapeDtypeStruct(query_shape, jnp.bfl...]
    ppermute x23, waiting for transfers between devices: 25.2 us -> 26.9 us  [moved(): return lax.ppermute(block, 'ctx', route)]
  transfers between devices with their start and end apart: 24 -> 24, of which waited for: 12 -> 14; matrix products, arithmetic and copies ran while one was open for 0% -> 1% of each run, Pallas kernels for 19% -> 16%
where the time goes in v1:
time: 90 us; the launch traced here: 90.1 us
  starting transfers between devices  41.8 us (46%)
  waiting for transfers between devices  26.9 us (30%)
  Pallas kernels  15.7 us (17%)
  local copies, waits for them, and re-layouts  4.42 us (5%)
    ppermute x23, starting transfers between devices, moved(): return lax.ppermute(block, 'ctx', route)  40.5 us
    ppermute x23, waiting for transfers between devices, moved(): return lax.ppermute(block, 'ctx', route)  26.9 us
    pallas_call x2, Pallas kernels, backward(): pl.pallas_call(body, out_shape=[jax.ShapeDtypeStruct(query_shape, jnp.bfl...  12.9 us
    unnamed x18, local copies, waits for them, and re-layouts  4.32 us
    pallas_call x6, Pallas kernels, small_call(): pl.pallas_call(kernel, out_shape=[jax.ShapeDtypeStruct(shape, jnp.bfloat1...  2.82 us
  transfers between devices with their start and end apart: 24, of which 14 were waited for; matrix products, arithmetic and copies ran while one was open for 1% of the time, Pallas kernels for 16%

profile of v1, /device:TPU:0, one launch (start us, length us, event | category | flops | bytes accessed | tf_op | source)
XLA Modules:
  0.0 90.1 jit_solution(15787485515932030670)
XLA Ops:
  0.6 0.9 %copy-done.5 = bf16[2,1,128,512]{3,2,1,0:T(8,128)(2,1)S(1)} copy-done((bf16[2,1,128,512]{3,2,1,0:T(8,128)(2,1)S(1)}, bf16[2,1,128,512]{3,2,1,0:T(8,128)(2,1)}, u32[]{:S(2)}) %copy-start.5) | copy-done | bytes 262168
  1.6 0.9 %copy-done.6 = bf16[2,1,128,512]{3,2,1,0:T(8,128)(2,1)S(1)} copy-done((bf16[2,1,128,512]{3,2,1,0:T(8,128)(2,1)S(1)}, bf16[2,1,128,512]{3,2,1,0:T(8,128)(2,1)}, u32[]{:S(2)}) %copy-start.6) | copy-done | bytes 262168
  2.6 3.0 %collective-permute-start = (bf16[2,128,512]{2,1,0:T(8,128)(2,1)S(1)}, bf16[2,128,512]{2,1,0:T(8,128)(2,1)S(1)}, u32[]{:S(2)}, u32[]{:S(2)}) collective-permute-start(bf16[2,128,512]{2,1,0:T(8,128)(2,1)S(1)} %get-tuple-element.33), channel_id=1, source_target_pairs={{0,1},{1,0},{2,3},{3,2},{4,5},{5,4},{6,7},{7,6},{8,9},{9,8},{10,11... | collective-permute-start | bytes 786440 | tf_op jit(solution)/shard_map/ppermute | solution.py:368
  5.6 1.3 %copy-done = bf16[2,1,128,2560]{3,2,1,0:T(8,128)(2,1)S(1)} copy-done((bf16[2,1,128,2560]{3,2,1,0:T(8,128)(2,1)S(1)}, bf16[2,1,128,2560]{3,2,1,0:T(8,128)(2,1)}, u32[]{:S(2)}) %copy-start) | copy-done | bytes 1310744
  6.9 1.1 %copy-done.2 = bf16[1,128,2560]{2,1,0:T(8,128)(2,1)S(1)} copy-done((bf16[1,128,2560]{2,1,0:T(8,128)(2,1)S(1)}, bf16[1,128,2560]{2,1,0:T(8,128)(2,1)}, u32[]{:S(2)}) %copy-start.2) | copy-done | bytes 655384
  8.1 0.1 collective-permute-start.1
  8.1 4.1 %collective-permute-start.3 = (bf16[128,512]{1,0:T(8,128)(2,1)S(1)}, bf16[128,512]{1,0:T(8,128)(2,1)S(1)}, u32[]{:S(2)}, u32[]{:S(2)}) collective-permute-start(bf16[128,512]{1,0:T(8,128)(2,1)S(1)} %get-tuple-element.34.refs_5_), channel_id=1, source_target_pairs={{0,6},{1,7},{2,4},{3,5},{4,2},{5,3},{6,0},{7,1},{8,14},{9,15},{10,... | collective-permute-start | bytes 393224 | tf_op jit(solution)/shard_map/ppermute | solution.py:368
  12.2 0.5 collective-permute-done
  12.8 4.2 %collective-permute-start.4 = (bf16[128,512]{1,0:T(8,128)(2,1)S(1)}, bf16[128,512]{1,0:T(8,128)(2,1)S(1)}, u32[]{:S(2)}, u32[]{:S(2)}) collective-permute-start(bf16[128,512]{1,0:T(8,128)(2,1)S(1)} %get-tuple-element.63.refs_6_), channel_id=1, source_target_pairs={{0,6},{1,7},{2,4},{3,5},{4,2},{5,3},{6,0},{7,1},{8,14},{9,15},{10,... | collective-permute-start | bytes 393224 | tf_op jit(solution)/shard_map/ppermute | solution.py:368
  17.0 0.0 collective-permute-start.2
  17.0 0.0 collective-permute-done.3.refs_7_
  17.0 4.1 %collective-permute-start.6 = (bf16[128,512]{1,0:T(8,128)(2,1)S(1)}, bf16[128,512]{1,0:T(8,128)(2,1)S(1)}, u32[]{:S(2)}, u32[]{:S(2)}) collective-permute-start(bf16[128,512]{1,0:T(8,128)(2,1)S(1)} %collective-permute-done.3.refs_7_), channel_id=1, source_target_pairs={{0,2},{1,3},{2,0},{3,1},{4,6},{5,7},{6,4},{7,5},{8,10},{9,11},{10,... | collective-permute-start | bytes 393224 | tf_op jit(solution)/shard_map/ppermute | solution.py:368
  21.1 0.0 collective-permute-start.5
  21.1 0.3 collective-permute-done.4.refs_8_
  21.4 1.9 %collective-permute-start.7 = (bf16[128,512]{1,0:T(8,128)(2,1)S(1)}, bf16[128,512]{1,0:T(8,128)(2,1)S(1)}, u32[]{:S(2)}, u32[]{:S(2)}) collective-permute-start(bf16[128,512]{1,0:T(8,128)(2,1)S(1)} %collective-permute-done.4.refs_8_), channel_id=1, source_target_pairs={{0,2},{1,3},{2,0},{3,1},{4,6},{5,7},{6,4},{7,5},{8,10},{9,11},{10,... | collective-permute-start | bytes 393224 | tf_op jit(solution)/shard_map/ppermute | solution.py:368
  23.4 0.0 copy-start.3
  23.4 0.0 copy-start.7
  23.4 0.0 copy-start.8
  23.4 0.1 shard_map.97
  23.5 0.4 collective-permute-done.2.refs_9_
  23.8 1.6 %collective-permute-start.10 = (bf16[2,128,1280]{2,1,0:T(8,128)(2,1)S(1)}, bf16[2,128,1280]{2,1,0:T(8,128)(2,1)S(1)}, u32[]{:S(2)}, u32[]{:S(2)}) collective-permute-start(bf16[2,128,1280]{2,1,0:T(8,128)(2,1)S(1)} %shard_map.97), channel_id=1, source_target_pairs={{0,1},{1,0},{2,3},{3,2},{4,5},{5,4},{6,7},{7,6},{8,9},{9,8},{10,11... | collective-permute-start | bytes 1966088 | tf_op jit(solution)/shard_map/ppermute | solution.py:368
  25.5 1.3 %collective-permute-done.1.refs_4_ = bf16[2,128,1280]{2,1,0:T(8,128)(2,1)S(1)} collective-permute-done((bf16[2,128,1280]{2,1,0:T(8,128)(2,1)S(1)}, bf16[2,128,1280]{2,1,0:T(8,128)(2,1)S(1)}, u32[]{:S(2)}, u32[]{:S(2)}) %collective-permute-start.1) | collective-permute-done | bytes 655392 | tf_op jit(solution)/shard_map/ppermute | solution.py:368
  26.8 4.1 %collective-permute-start.8 = (bf16[2,128,512]{2,1,0:T(8,128)(2,1)S(1)}, bf16[2,128,512]{2,1,0:T(8,128)(2,1)S(1)}, u32[]{:S(2)}, u32[]{:S(2)}) collective-permute-start(bf16[2,128,512]{2,1,0:T(8,128)(2,1)S(1)} %pad_maximum_fusion.refs_6_), channel_id=1, source_target_pairs={{0,6},{1,7},{2,4},{3,5},{4,2},{5,3},{6,0},{7,1},{8,14},{9,15},{10,... | collective-permute-start | bytes 786440 | tf_op jit(solution)/shard_map/ppermute | solution.py:368
  30.9 0.0 collective-permute-done.6.refs_11_
  30.9 0.0 collective-permute-start.9
  30.9 0.0 collective-permute-done.5.refs_10_
  30.9 0.0 collective-permute-done.7.refs_12_
  31.0 8.6 %shard_map.96 = (bf16[2,128,1280]{2,1,0:T(8,128)(2,1)S(1)}, bf16[2,128,512]{2,1,0:T(8,128)(2,1)S(1)}, bf16[2,128,512]{2,1,0:T(8,128)(2,1)S(1)}, bf16[2,128,512]{2,1,0:T(8,128)(2,1)S(1)}, bf16[2,128,512]{2,1,0:T(8,128)(2,1)S(1)}) custom-call(s32[2,1,8,8]{3,2,1,0:T(8,128)S(1)} %copy-done.7, s32[2,1,8]{2,1,0:T(1,128)S(1)} %copy-done.8, ...), custom_call_target="tpu_custom_call" | custom-call | flops 10000000000 | bytes 4000000 | tf_op jit(solution)/shard_map/pallas_call | solution.py:274
  39.6 0.0 collective-permute-done.8.refs_7_
  39.6 1.9 %collective-permute-done.9.refs_8_ = bf16[2,128,512]{2,1,0:T(8,128)(2,1)S(1)} collective-permute-done((bf16[2,128,512]{2,1,0:T(8,128)(2,1)S(1)}, bf16[2,128,512]{2,1,0:T(8,128)(2,1)S(1)}, u32[]{:S(2)}, u32[]{:S(2)}) %collective-permute-start.9) | collective-permute-done | bytes 262176 | tf_op jit(solution)/shard_map/ppermute | solution.py:368
  41.5 1.6 %collective-permute-start.15 = (bf16[2,128,512]{2,1,0:T(8,128)(2,1)S(1)}, bf16[2,128,512]{2,1,0:T(8,128)(2,1)S(1)}, u32[]{:S(2)}, u32[]{:S(2)}) collective-permute-start(bf16[2,128,512]{2,1,0:T(8,128)(2,1)S(1)} %get-tuple-element.49), channel_id=1, source_target_pairs={{0,2},{1,3},{2,0},{3,1},{4,6},{5,7},{6,4},{7,5},{8,10},{9,11},{10,... | collective-permute-start | bytes 786440 | tf_op jit(solution)/shard_map/ppermute | solution.py:368
  43.0 1.3 %collective-permute-start.11 = (bf16[2,128,1280]{2,1,0:T(8,128)(2,1)S(1)}, bf16[2,128,1280]{2,1,0:T(8,128)(2,1)S(1)}, u32[]{:S(2)}, u32[]{:S(2)}) collective-permute-start(bf16[2,128,1280]{2,1,0:T(8,128)(2,1)S(1)} %get-tuple-element.42.own_ref), channel_id=1, source_target_pairs={{8,0},{16,8},{24,16},{9,1},{17,9},{25,17},{10,2},{18,10},{26,18},{... | collective-permute-start | bytes 1966088 | tf_op jit(solution)/shard_map/ppermute | solution.py:374
  44.3 0.5 collective-permute-start.12
  44.9 1.6 %collective-permute-start.14 = (bf16[128,1280]{1,0:T(8,128)(2,1)S(1)}, bf16[128,1280]{1,0:T(8,128)(2,1)S(1)}, u32[]{:S(2)}, u32[]{:S(2)}) collective-permute-start(bf16[128,1280]{1,0:T(8,128)(2,1)S(1)} %slice_bitcast_fusion.1), channel_id=1, source_target_pairs={{0,1},{1,0},{2,3},{3,2},{4,5},{5,4},{6,7},{7,6},{8,9},{9,8},{10,11... | collective-permute-start | bytes 983048 | tf_op jit(solution)/shard_map/ppermute | solution.py:368
  46.4 3.8 %collective-permute-done.15 = bf16[2,128,512]{2,1,0:T(8,128)(2,1)S(1)} collective-permute-done((bf16[2,128,512]{2,1,0:T(8,128)(2,1)S(1)}, bf16[2,128,512]{2,1,0:T(8,128)(2,1)S(1)}, u32[]{:S(2)}, u32[]{:S(2)}) %collective-permute-start.15) | collective-permute-done | bytes 262176 | tf_op jit(solution)/shard_map/ppermute | solution.py:368
  50.3 0.1 collective-permute-start.17
  50.4 0.1 add_convert_fusion.3
  50.5 0.0 collective-permute-done.10.refs_4_
  50.5 3.0 %collective-permute-start.16 = (bf16[2,128,512]{2,1,0:T(8,128)(2,1)S(1)}, bf16[2,128,512]{2,1,0:T(8,128)(2,1)S(1)}, u32[]{:S(2)}, u32[]{:S(2)}) collective-permute-start(bf16[2,128,512]{2,1,0:T(8,128)(2,1)S(1)} %add_convert_fusion.3), channel_id=1, source_target_pairs={{0,6},{1,7},{2,4},{3,5},{4,2},{5,3},{6,0},{7,1},{8,14},{9,15},{10,... | collective-permute-start | bytes 786440 | tf_op jit(solution)/shard_map/ppermute | solution.py:368
  53.5 2.4 %collective-permute-done.12.refs_9_ = bf16[2,128,512]{2,1,0:T(8,128)(2,1)S(1)} collective-permute-done((bf16[2,128,512]{2,1,0:T(8,128)(2,1)S(1)}, bf16[2,128,512]{2,1,0:T(8,128)(2,1)S(1)}, u32[]{:S(2)}, u32[]{:S(2)}) %collective-permute-start.12) | collective-permute-done | bytes 262176 | tf_op jit(solution)/shard_map/ppermute | solution.py:368
  55.9 0.0 collective-permute-done.11.refs_5_
  55.9 4.3 %shard_map.98 = (bf16[2,128,1280]{2,1,0:T(8,128)(2,1)S(1)}, bf16[2,128,512]{2,1,0:T(8,128)(2,1)S(1)}, bf16[2,128,512]{2,1,0:T(8,128)(2,1)S(1)}, bf16[2,128,512]{2,1,0:T(8,128)(2,1)S(1)}, bf16[2,128,512]{2,1,0:T(8,128)(2,1)S(1)}) custom-call(s32[2,1,8,8]{3,2,1,0:T(8,128)S(1)} %copy-done.7, s32[2,1,8]{2,1,0:T(1,128)S(1)} %copy-done.8, ...), custom_call_target="tpu_custom_call" | custom-call | flops 10000000000 | bytes 4000000 | tf_op jit(solution)/shard_map/pallas_call | solution.py:274
  60.2 0.2 collective-permute-start.13
  60.4 1.9 %collective-permute-start.20 = (bf16[2,128,512]{2,1,0:T(8,128)(2,1)S(1)}, bf16[2,128,512]{2,1,0:T(8,128)(2,1)S(1)}, u32[]{:S(2)}, u32[]{:S(2)}) collective-permute-start(bf16[2,128,512]{2,1,0:T(8,128)(2,1)S(1)} %get-tuple-element.58), channel_id=1, source_target_pairs={{0,2},{1,3},{2,0},{3,1},{4,6},{5,7},{6,4},{7,5},{8,10},{9,11},{10,... | collective-permute-start | bytes 786440 | tf_op jit(solution)/shard_map/ppermute | solution.py:368
  62.3 0.0 collective-permute-done.17
  62.3 1.4 %collective-permute-start.18 = (bf16[128,1280]{1,0:T(8,128)(2,1)S(1)}, bf16[128,1280]{1,0:T(8,128)(2,1)S(1)}, u32[]{:S(2)}, u32[]{:S(2)}) collective-permute-start(bf16[128,1280]{1,0:T(8,128)(2,1)S(1)} %slice_bitcast_fusion), channel_id=1, source_target_pairs={{0,1},{1,0},{2,3},{3,2},{4,5},{5,4},{6,7},{7,6},{8,9},{9,8},{10,11... | collective-permute-start | bytes 983048 | tf_op jit(solution)/shard_map/ppermute | solution.py:368
  63.7 0.0 collective-permute-done.14.received_ref
  63.7 3.1 %collective-permute-done.16 = bf16[2,128,512]{2,1,0:T(8,128)(2,1)S(1)} collective-permute-done((bf16[2,128,512]{2,1,0:T(8,128)(2,1)S(1)}, bf16[2,128,512]{2,1,0:T(8,128)(2,1)S(1)}, u32[]{:S(2)}, u32[]{:S(2)}) %collective-permute-start.16) | collective-permute-done | bytes 262176 | tf_op jit(solution)/shard_map/ppermute | solution.py:368
  66.8 5.5 %collective-permute-done.13 = bf16[2,128,512]{2,1,0:T(8,128)(2,1)S(1)} collective-permute-done((bf16[2,128,512]{2,1,0:T(8,128)(2,1)S(1)}, bf16[2,128,512]{2,1,0:T(8,128)(2,1)S(1)}, u32[]{:S(2)}, u32[]{:S(2)}) %collective-permute-start.13) | collective-permute-done | bytes 262176 | tf_op jit(solution)/shard_map/ppermute | solution.py:368
  72.3 0.1 add_convert_fusion
  72.4 2.0 %collective-permute-start.21 = (bf16[128,512]{1,0:T(8,128)(2,1)S(1)}, bf16[128,512]{1,0:T(8,128)(2,1)S(1)}, u32[]{:S(2)}, u32[]{:S(2)}) collective-permute-start(bf16[128,512]{1,0:T(8,128)(2,1)S(1)} %get-tuple-element.62), channel_id=1, source_target_pairs={{0,6},{1,7},{2,4},{3,5},{4,2},{5,3},{6,0},{7,1},{8,14},{9,15},{10,... | collective-permute-start | bytes 393224 | tf_op jit(solution)/shard_map/ppermute | solution.py:368
  74.4 2.8 %collective-permute-start.22 = (bf16[128,512]{1,0:T(8,128)(2,1)S(1)}, bf16[128,512]{1,0:T(8,128)(2,1)S(1)}, u32[]{:S(2)}, u32[]{:S(2)}) collective-permute-start(bf16[128,512]{1,0:T(8,128)(2,1)S(1)} %get-tuple-element.61), channel_id=1, source_target_pairs={{0,7},{1,6},{2,5},{3,4},{4,3},{5,2},{6,1},{7,0},{8,15},{9,14},{10,... | collective-permute-start | bytes 393224 | tf_op jit(solution)/shard_map/ppermute | solution.py:368
  77.3 0.7 collective-permute-done.20
  77.9 0.1 add_convert_fusion.1.local_ref
  78.0 1.6 %collective-permute-start.23 = (bf16[128,512]{1,0:T(8,128)(2,1)S(1)}, bf16[128,512]{1,0:T(8,128)(2,1)S(1)}, u32[]{:S(2)}, u32[]{:S(2)}) collective-permute-start(bf16[128,512]{1,0:T(8,128)(2,1)S(1)} %slice_bitcast_fusion.2), channel_id=1, source_target_pairs={{0,1},{1,0},{2,3},{3,2},{4,5},{5,4},{6,7},{7,6},{8,9},{9,8},{10,11... | collective-permute-start | bytes 393224 | tf_op jit(solution)/shard_map/ppermute | solution.py:368
  79.6 0.1 add_convert_fusion.2.sum_ref
  79.7 0.6 collective-permute-start.19
  80.3 0.9 %shard_map.99 = bf16[1,128,2560]{2,1,0:T(8,128)(2,1)} custom-call(bf16[2,128,1280]{2,1,0:T(8,128)(2,1)S(1)} %get-tuple-element.42.own_ref, bf16[128,1280]{1,0:T(8,128)(2,1)S(1)} %collective-permute-done.14.received_ref), custom_call_target="tpu_custom_call" | custom-call | bytes 1966080 | tf_op jit(solution)/shard_map/pallas_call | solution.py:300
  81.2 0.9 %shard_map.100 = bf16[1,128,2560]{2,1,0:T(8,128)(2,1)} custom-call(bf16[2,128,1280]{2,1,0:T(8,128)(2,1)S(1)} %get-tuple-element.53.own_ref, bf16[128,1280]{1,0:T(8,128)(2,1)S(1)} %collective-permute-done.18.received_ref), custom_call_target="tpu_custom_call" | custom-call | bytes 1966080 | tf_op jit(solution)/shard_map/pallas_call | solution.py:300
  82.1 0.6 collective-permute-done.21.refs_0_
  82.8 3.9 %collective-permute-done.22.refs_1_ = bf16[128,512]{1,0:T(8,128)(2,1)S(1)} collective-permute-done((bf16[128,512]{1,0:T(8,128)(2,1)S(1)}, bf16[128,512]{1,0:T(8,128)(2,1)S(1)}, u32[]{:S(2)}, u32[]{:S(2)}) %collective-permute-start.22) | collective-permute-done | bytes 131104 | tf_op jit(solution)/shard_map/ppermute | solution.py:368
  86.6 0.6 collective-permute-done.23.refs_2_
  87.3 2.0 %collective-permute-done.19.crossed_ref = bf16[128,512]{1,0:T(8,128)(2,1)S(1)} collective-permute-done((bf16[128,512]{1,0:T(8,128)(2,1)S(1)}, bf16[128,512]{1,0:T(8,128)(2,1)S(1)}, u32[]{:S(2)}, u32[]{:S(2)}) %collective-permute-start.19) | collective-permute-done | bytes 131104 | tf_op jit(solution)/shard_map/ppermute | solution.py:368
  89.2 0.9 shard_map.101
  (21 shorter events, 0.2 us)
Async XLA Ops:
  0.6 1.0 %copy-start.5 = (bf16[2,1,128,512]{3,2,1,0:T(8,128)(2,1)S(1)}, bf16[2,1,128,512]{3,2,1,0:T(8,128)(2,1)}, u32[]{:S(2)}) copy-start(bf16[2,1,128,512]{3,2,1,0:T(8,128)(2,1)} %key_ref.1) | copy-start | bytes 786436
  1.6 0.9 %copy-start.6 = (bf16[2,1,128,512]{3,2,1,0:T(8,128)(2,1)S(1)}, bf16[2,1,128,512]{3,2,1,0:T(8,128)(2,1)}, u32[]{:S(2)}) copy-start(bf16[2,1,128,512]{3,2,1,0:T(8,128)(2,1)} %value_ref.1) | copy-start | bytes 786436
  2.6 10.2 %collective-permute-start = (bf16[2,128,512]{2,1,0:T(8,128)(2,1)S(1)}, bf16[2,128,512]{2,1,0:T(8,128)(2,1)S(1)}, u32[]{:S(2)}, u32[]{:S(2)}) collective-permute-start(bf16[2,128,512]{2,1,0:T(8,128)(2,1)S(1)} %get-tuple-element.33), channel_id=1, source_target_pairs={{0,1},{1,0},{2,3},{3,2},{4,5},{5,4},{6,7},{7,6},{8,9},{9,8},{10,11... | collective-permute-start | bytes 786440 | tf_op jit(solution)/shard_map/ppermute | solution.py:368
  5.6 1.3 %copy-start = (bf16[2,1,128,2560]{3,2,1,0:T(8,128)(2,1)S(1)}, bf16[2,1,128,2560]{3,2,1,0:T(8,128)(2,1)}, u32[]{:S(2)}) copy-start(bf16[2,1,128,2560]{3,2,1,0:T(8,128)(2,1)} %refs_2_.3) | copy-start | bytes 3932164
  6.9 1.1 %copy-start.2 = (bf16[1,128,2560]{2,1,0:T(8,128)(2,1)S(1)}, bf16[1,128,2560]{2,1,0:T(8,128)(2,1)}, u32[]{:S(2)}) copy-start(bf16[1,128,2560]{2,1,0:T(8,128)(2,1)} %refs_3_.2) | copy-start | bytes 1966084
  8.0 15.3 %copy-start.1 = (bf16[2,1,128,2560]{3,2,1,0:T(8,128)(2,1)S(1)}, bf16[2,1,128,2560]{3,2,1,0:T(8,128)(2,1)}, u32[]{:S(2)}) copy-start(bf16[2,1,128,2560]{3,2,1,0:T(8,128)(2,1)} %refs_2_.3) | copy-start | bytes 3932164
  8.0 15.3 %copy-start.4 = (bf16[1,128,2560]{2,1,0:T(8,128)(2,1)S(1)}, bf16[1,128,2560]{2,1,0:T(8,128)(2,1)}, u32[]{:S(2)}) copy-start(bf16[1,128,2560]{2,1,0:T(8,128)(2,1)} %refs_3_.3) | copy-start | bytes 1966084
  8.1 18.7 %collective-permute-start.1 = (bf16[2,128,1280]{2,1,0:T(8,128)(2,1)S(1)}, bf16[2,128,1280]{2,1,0:T(8,128)(2,1)S(1)}, u32[]{:S(2)}, u32[]{:S(2)}) collective-permute-start(bf16[2,128,1280]{2,1,0:T(8,128)(2,1)S(1)} %shard_map.95), channel_id=1, source_target_pairs={{0,1},{1,0},{2,3},{3,2},{4,5},{5,4},{6,7},{7,6},{8,9},{9,8},{10,11... | collective-permute-start | bytes 1966088 | tf_op jit(solution)/shard_map/ppermute | solution.py:368
  8.1 8.8 %collective-permute-start.3 = (bf16[128,512]{1,0:T(8,128)(2,1)S(1)}, bf16[128,512]{1,0:T(8,128)(2,1)S(1)}, u32[]{:S(2)}, u32[]{:S(2)}) collective-permute-start(bf16[128,512]{1,0:T(8,128)(2,1)S(1)} %get-tuple-element.34.refs_5_), channel_id=1, source_target_pairs={{0,6},{1,7},{2,4},{3,5},{4,2},{5,3},{6,0},{7,1},{8,14},{9,15},{10,... | collective-permute-start | bytes 393224 | tf_op jit(solution)/shard_map/ppermute | solution.py:368
  12.8 8.6 %collective-permute-start.4 = (bf16[128,512]{1,0:T(8,128)(2,1)S(1)}, bf16[128,512]{1,0:T(8,128)(2,1)S(1)}, u32[]{:S(2)}, u32[]{:S(2)}) collective-permute-start(bf16[128,512]{1,0:T(8,128)(2,1)S(1)} %get-tuple-element.63.refs_6_), channel_id=1, source_target_pairs={{0,6},{1,7},{2,4},{3,5},{4,2},{5,3},{6,0},{7,1},{8,14},{9,15},{10,... | collective-permute-start | bytes 393224 | tf_op jit(solution)/shard_map/ppermute | solution.py:368
  17.0 6.9 %collective-permute-start.2 = (bf16[128,512]{1,0:T(8,128)(2,1)S(1)}, bf16[128,512]{1,0:T(8,128)(2,1)S(1)}, u32[]{:S(2)}, u32[]{:S(2)}) collective-permute-start(bf16[128,512]{1,0:T(8,128)(2,1)S(1)} %get-tuple-element.34.refs_5_), channel_id=1, source_target_pairs={{0,2},{1,3},{2,0},{3,1},{4,6},{5,7},{6,4},{7,5},{8,10},{9,11},{10,... | collective-permute-start | bytes 393224 | tf_op jit(solution)/shard_map/ppermute | solution.py:368
  17.0 14.0 %collective-permute-start.6 = (bf16[128,512]{1,0:T(8,128)(2,1)S(1)}, bf16[128,512]{1,0:T(8,128)(2,1)S(1)}, u32[]{:S(2)}, u32[]{:S(2)}) collective-permute-start(bf16[128,512]{1,0:T(8,128)(2,1)S(1)} %collective-permute-done.3.refs_7_), channel_id=1, source_target_pairs={{0,2},{1,3},{2,0},{3,1},{4,6},{5,7},{6,4},{7,5},{8,10},{9,11},{10,... | collective-permute-start | bytes 393224 | tf_op jit(solution)/shard_map/ppermute | solution.py:368
  21.1 9.9 %collective-permute-start.5 = (bf16[128,512]{1,0:T(8,128)(2,1)S(1)}, bf16[128,512]{1,0:T(8,128)(2,1)S(1)}, u32[]{:S(2)}, u32[]{:S(2)}) collective-permute-start(bf16[128,512]{1,0:T(8,128)(2,1)S(1)} %get-tuple-element.63.refs_6_), channel_id=1, source_target_pairs={{0,2},{1,3},{2,0},{3,1},{4,6},{5,7},{6,4},{7,5},{8,10},{9,11},{10,... | collective-permute-start | bytes 393224 | tf_op jit(solution)/shard_map/ppermute | solution.py:368
  21.4 9.6 %collective-permute-start.7 = (bf16[128,512]{1,0:T(8,128)(2,1)S(1)}, bf16[128,512]{1,0:T(8,128)(2,1)S(1)}, u32[]{:S(2)}, u32[]{:S(2)}) collective-permute-start(bf16[128,512]{1,0:T(8,128)(2,1)S(1)} %collective-permute-done.4.refs_8_), channel_id=1, source_target_pairs={{0,2},{1,3},{2,0},{3,1},{4,6},{5,7},{6,4},{7,5},{8,10},{9,11},{10,... | collective-permute-start | bytes 393224 | tf_op jit(solution)/shard_map/ppermute | solution.py:368
  23.4 7.6 %copy-start.3 = (bf16[1,128,2560]{2,1,0:T(8,128)(2,1)S(1)}, bf16[1,128,2560]{2,1,0:T(8,128)(2,1)}, u32[]{:S(2)}) copy-start(bf16[1,128,2560]{2,1,0:T(8,128)(2,1)} %refs_3_.2) | copy-start | bytes 1966084
  23.4 7.6 %copy-start.7 = (s32[2,1,8,8]{3,2,1,0:T(8,128)S(1)}, s32[2,1,8,8]{3,2,1,0:T(8,128)}, u32[]{:S(2)}) copy-start(s32[2,1,8,8]{3,2,1,0:T(8,128)} %refs_0_.6) | copy-start | bytes 1540
  23.4 7.6 %copy-start.8 = (s32[2,1,8]{2,1,0:T(1,128)S(1)}, s32[2,1,8]{2,1,0:T(1,128)}, u32[]{:S(2)}) copy-start(s32[2,1,8]{2,1,0:T(1,128)} %refs_1_.6) | copy-start | bytes 196
  23.8 26.7 %collective-permute-start.10 = (bf16[2,128,1280]{2,1,0:T(8,128)(2,1)S(1)}, bf16[2,128,1280]{2,1,0:T(8,128)(2,1)S(1)}, u32[]{:S(2)}, u32[]{:S(2)}) collective-permute-start(bf16[2,128,1280]{2,1,0:T(8,128)(2,1)S(1)} %shard_map.97), channel_id=1, source_target_pairs={{0,1},{1,0},{2,3},{3,2},{4,5},{5,4},{6,7},{7,6},{8,9},{9,8},{10,11... | collective-permute-start | bytes 1966088 | tf_op jit(solution)/shard_map/ppermute | solution.py:368
  26.8 12.8 %collective-permute-start.8 = (bf16[2,128,512]{2,1,0:T(8,128)(2,1)S(1)}, bf16[2,128,512]{2,1,0:T(8,128)(2,1)S(1)}, u32[]{:S(2)}, u32[]{:S(2)}) collective-permute-start(bf16[2,128,512]{2,1,0:T(8,128)(2,1)S(1)} %pad_maximum_fusion.refs_6_), channel_id=1, source_target_pairs={{0,6},{1,7},{2,4},{3,5},{4,2},{5,3},{6,0},{7,1},{8,14},{9,15},{10,... | collective-permute-start | bytes 786440 | tf_op jit(solution)/shard_map/ppermute | solution.py:368
  30.9 10.5 %collective-permute-start.9 = (bf16[2,128,512]{2,1,0:T(8,128)(2,1)S(1)}, bf16[2,128,512]{2,1,0:T(8,128)(2,1)S(1)}, u32[]{:S(2)}, u32[]{:S(2)}) collective-permute-start(bf16[2,128,512]{2,1,0:T(8,128)(2,1)S(1)} %pad_maximum_fusion.refs_6_), channel_id=1, source_target_pairs={{0,2},{1,3},{2,0},{3,1},{4,6},{5,7},{6,4},{7,5},{8,10},{9,11},{10,... | collective-permute-start | bytes 786440 | tf_op jit(solution)/shard_map/ppermute | solution.py:368
  41.5 8.8 %collective-permute-start.15 = (bf16[2,128,512]{2,1,0:T(8,128)(2,1)S(1)}, bf16[2,128,512]{2,1,0:T(8,128)(2,1)S(1)}, u32[]{:S(2)}, u32[]{:S(2)}) collective-permute-start(bf16[2,128,512]{2,1,0:T(8,128)(2,1)S(1)} %get-tuple-element.49), channel_id=1, source_target_pairs={{0,2},{1,3},{2,0},{3,1},{4,6},{5,7},{6,4},{7,5},{8,10},{9,11},{10,... | collective-permute-start | bytes 786440 | tf_op jit(solution)/shard_map/ppermute | solution.py:368
  43.0 12.8 %collective-permute-start.11 = (bf16[2,128,1280]{2,1,0:T(8,128)(2,1)S(1)}, bf16[2,128,1280]{2,1,0:T(8,128)(2,1)S(1)}, u32[]{:S(2)}, u32[]{:S(2)}) collective-permute-start(bf16[2,128,1280]{2,1,0:T(8,128)(2,1)S(1)} %get-tuple-element.42.own_ref), channel_id=1, source_target_pairs={{8,0},{16,8},{24,16},{9,1},{17,9},{25,17},{10,2},{18,10},{26,18},{... | collective-permute-start | bytes 1966088 | tf_op jit(solution)/shard_map/ppermute | solution.py:374
  44.3 11.6 %collective-permute-start.12 = (bf16[2,128,512]{2,1,0:T(8,128)(2,1)S(1)}, bf16[2,128,512]{2,1,0:T(8,128)(2,1)S(1)}, u32[]{:S(2)}, u32[]{:S(2)}) collective-permute-start(bf16[2,128,512]{2,1,0:T(8,128)(2,1)S(1)} %collective-permute-done.8.refs_7_), channel_id=1, source_target_pairs={{0,2},{1,3},{2,0},{3,1},{4,6},{5,7},{6,4},{7,5},{8,10},{9,11},{10,... | collective-permute-start | bytes 786440 | tf_op jit(solution)/shard_map/ppermute | solution.py:368
  44.9 18.9 %collective-permute-start.14 = (bf16[128,1280]{1,0:T(8,128)(2,1)S(1)}, bf16[128,1280]{1,0:T(8,128)(2,1)S(1)}, u32[]{:S(2)}, u32[]{:S(2)}) collective-permute-start(bf16[128,1280]{1,0:T(8,128)(2,1)S(1)} %slice_bitcast_fusion.1), channel_id=1, source_target_pairs={{0,1},{1,0},{2,3},{3,2},{4,5},{5,4},{6,7},{7,6},{8,9},{9,8},{10,11... | collective-permute-start | bytes 983048 | tf_op jit(solution)/shard_map/ppermute | solution.py:368
  50.3 12.1 %collective-permute-start.17 = (bf16[2,128,512]{2,1,0:T(8,128)(2,1)S(1)}, bf16[2,128,512]{2,1,0:T(8,128)(2,1)S(1)}, u32[]{:S(2)}, u32[]{:S(2)}) collective-permute-start(bf16[2,128,512]{2,1,0:T(8,128)(2,1)S(1)} %get-tuple-element.51), channel_id=1, source_target_pairs={{0,2},{1,3},{2,0},{3,1},{4,6},{5,7},{6,4},{7,5},{8,10},{9,11},{10,... | collective-permute-start | bytes 786440 | tf_op jit(solution)/shard_map/ppermute | solution.py:368
  50.5 16.3 %collective-permute-start.16 = (bf16[2,128,512]{2,1,0:T(8,128)(2,1)S(1)}, bf16[2,128,512]{2,1,0:T(8,128)(2,1)S(1)}, u32[]{:S(2)}, u32[]{:S(2)}) collective-permute-start(bf16[2,128,512]{2,1,0:T(8,128)(2,1)S(1)} %add_convert_fusion.3), channel_id=1, source_target_pairs={{0,6},{1,7},{2,4},{3,5},{4,2},{5,3},{6,0},{7,1},{8,14},{9,15},{10,... | collective-permute-start | bytes 786440 | tf_op jit(solution)/shard_map/ppermute | solution.py:368
  60.2 12.1 %collective-permute-start.13 = (bf16[2,128,512]{2,1,0:T(8,128)(2,1)S(1)}, bf16[2,128,512]{2,1,0:T(8,128)(2,1)S(1)}, u32[]{:S(2)}, u32[]{:S(2)}) collective-permute-start(bf16[2,128,512]{2,1,0:T(8,128)(2,1)S(1)} %get-tuple-element.47), channel_id=1, source_target_pairs={{0,2},{1,3},{2,0},{3,1},{4,6},{5,7},{6,4},{7,5},{8,10},{9,11},{10,... | collective-permute-start | bytes 786440 | tf_op jit(solution)/shard_map/ppermute | solution.py:368
  60.4 17.5 %collective-permute-start.20 = (bf16[2,128,512]{2,1,0:T(8,128)(2,1)S(1)}, bf16[2,128,512]{2,1,0:T(8,128)(2,1)S(1)}, u32[]{:S(2)}, u32[]{:S(2)}) collective-permute-start(bf16[2,128,512]{2,1,0:T(8,128)(2,1)S(1)} %get-tuple-element.58), channel_id=1, source_target_pairs={{0,2},{1,3},{2,0},{3,1},{4,6},{5,7},{6,4},{7,5},{8,10},{9,11},{10,... | collective-permute-start | bytes 786440 | tf_op jit(solution)/shard_map/ppermute | solution.py:368
  62.3 18.9 %collective-permute-start.18 = (bf16[128,1280]{1,0:T(8,128)(2,1)S(1)}, bf16[128,1280]{1,0:T(8,128)(2,1)S(1)}, u32[]{:S(2)}, u32[]{:S(2)}) collective-permute-start(bf16[128,1280]{1,0:T(8,128)(2,1)S(1)} %slice_bitcast_fusion), channel_id=1, source_target_pairs={{0,1},{1,0},{2,3},{3,2},{4,5},{5,4},{6,7},{7,6},{8,9},{9,8},{10,11... | collective-permute-start | bytes 983048 | tf_op jit(solution)/shard_map/ppermute | solution.py:368
  72.4 10.3 %collective-permute-start.21 = (bf16[128,512]{1,0:T(8,128)(2,1)S(1)}, bf16[128,512]{1,0:T(8,128)(2,1)S(1)}, u32[]{:S(2)}, u32[]{:S(2)}) collective-permute-start(bf16[128,512]{1,0:T(8,128)(2,1)S(1)} %get-tuple-element.62), channel_id=1, source_target_pairs={{0,6},{1,7},{2,4},{3,5},{4,2},{5,3},{6,0},{7,1},{8,14},{9,15},{10,... | collective-permute-start | bytes 393224 | tf_op jit(solution)/shard_map/ppermute | solution.py:368
  74.4 12.2 %collective-permute-start.22 = (bf16[128,512]{1,0:T(8,128)(2,1)S(1)}, bf16[128,512]{1,0:T(8,128)(2,1)S(1)}, u32[]{:S(2)}, u32[]{:S(2)}) collective-permute-start(bf16[128,512]{1,0:T(8,128)(2,1)S(1)} %get-tuple-element.61), channel_id=1, source_target_pairs={{0,7},{1,6},{2,5},{3,4},{4,3},{5,2},{6,1},{7,0},{8,15},{9,14},{10,... | collective-permute-start | bytes 393224 | tf_op jit(solution)/shard_map/ppermute | solution.py:368
  78.0 9.2 %collective-permute-start.23 = (bf16[128,512]{1,0:T(8,128)(2,1)S(1)}, bf16[128,512]{1,0:T(8,128)(2,1)S(1)}, u32[]{:S(2)}, u32[]{:S(2)}) collective-permute-start(bf16[128,512]{1,0:T(8,128)(2,1)S(1)} %slice_bitcast_fusion.2), channel_id=1, source_target_pairs={{0,1},{1,0},{2,3},{3,2},{4,5},{5,4},{6,7},{7,6},{8,9},{9,8},{10,11... | collective-permute-start | bytes 393224 | tf_op jit(solution)/shard_map/ppermute | solution.py:368
  79.7 9.5 %collective-permute-start.19 = (bf16[128,512]{1,0:T(8,128)(2,1)S(1)}, bf16[128,512]{1,0:T(8,128)(2,1)S(1)}, u32[]{:S(2)}, u32[]{:S(2)}) collective-permute-start(bf16[128,512]{1,0:T(8,128)(2,1)S(1)} %slice_bitcast_fusion.5), channel_id=1, source_target_pairs={{0,1},{1,0},{2,3},{3,2},{4,5},{5,4},{6,7},{7,6},{8,9},{9,8},{10,11... | collective-permute-start | bytes 393224 | tf_op jit(solution)/shard_map/ppermute | solution.py:368
